TPU v7x, 512 devices: a whole 4x8x8 slice. The times are simulated.
512 devices in a mesh: pairs: 128 (over x, z, y_hi, core), tm: 4 (over y_lo).
Axes of the slice: x: 4, y: 8 (y_hi: 2, y_lo: 4; y = y_hi * 4 + y_lo), z: 8, core: 2. Of those that a mesh axis runs over, the one named last changes fastest.
Arguments:
- records: bfloat16 [4, 512, 2048], P('tm', 'pairs'), may hold values from -50 to 50
- alive: int32 [512], P('pairs'), may hold values 0 or 1
- tile_block: int32 [128], P('pairs'), may hold values from 0 to 1
Outputs:
- stack: bfloat16 [512, 512, 256], P('tm', 'pairs')
All inputs are finite; a program needn't handle non-finite values. No bound on the sum of `alive` on one device may be relied on, other than what follows from the above.
Results may differ from a plain program's by a relative error of at most 0.013.
Values may be sent and summed in bfloat16 or wider, within the bound.
No kernel may reach another device: no remote copies, remote signals or barrier semaphores. Data moves between devices by JAX's collectives and lax.ppermute only.
A program may use at most 64 MiB of HBM per device.

v0:
```python
import jax
import jax.numpy as jnp
from jax import lax
from jax.sharding import PartitionSpec as P

LAGS = 512
NBLK = 2


def normalize(records, alive):
    data = records.astype(jnp.float32)
    power = jnp.mean(data * data, axis=-1, keepdims=True)
    scaled = data * lax.rsqrt(power + 1e-05) * alive[None, :, None].astype(jnp.float32)
    return scaled.astype(jnp.bfloat16)


def lagged_products(own_rows, columns, lag_first, count):
    rows, samples = own_rows.shape
    span = LAGS
    blocks = samples // span
    width = span + count
    padded = jnp.pad(columns, ((0, 0), (LAGS // 2, span + count)))

    def one_block(total, index):
        start = index * span
        piece = lax.dynamic_slice_in_dim(own_rows, start, span, 1)
        extended = jnp.pad(piece, ((0, 0), (0, count + 1)))
        skewed = jnp.tile(extended, (1, count))[:, : count * width].reshape(rows * count, width)
        window = lax.dynamic_slice_in_dim(padded, start + lag_first, width, 1)
        part_sum = lax.dot_general(
            skewed, window, (((1,), (1,)), ((), ())), preferred_element_type=jnp.float32
        )
        return (total + part_sum, None)

    empty = jnp.zeros((rows * count, columns.shape[0]), jnp.float32)
    total, _ = lax.scan(one_block, empty, jnp.arange(blocks, dtype=jnp.int32))
    return jnp.transpose(total.reshape(rows, count, columns.shape[0]), (1, 0, 2))


def local(records, alive, tile_block):
    normal = normalize(records, alive)
    rows = normal.shape[1]
    channels = rows * lax.axis_size("pairs")
    block_width = channels // NBLK
    block_first = tile_block[0] * block_width
    segments = lax.axis_size("tm") * records.shape[0]
    gathered = lax.all_gather(normal, "pairs", axis=1, tiled=True)
    block = lax.dynamic_slice_in_dim(gathered[0], block_first, block_width, 0)
    terms = lagged_products(normal[0], block, 0, LAGS)
    summed = lax.psum_scatter(
        terms.astype(jnp.bfloat16), "tm", scatter_dimension=0, tiled=True
    ).astype(jnp.float32)
    return (summed / segments).astype(jnp.bfloat16)


def solution(mesh):
    in_specs = (P("tm", "pairs", None), P("pairs"), P("pairs"))
    out_specs = P("tm", "pairs", None)
    return jax.shard_map(local, mesh=mesh, in_specs=in_specs, out_specs=out_specs, check_vma=False)
```

profile of v0, /device:TPU:1, one launch (start us, length us, event | category | flops | bytes accessed | tf_op | source)
XLA Modules:
  0.0 337.0 jit_solution(3310393560267110374)
XLA Ops:
  6.5 0.0 all-gather.2.cloned.1.call-start
  6.5 0.7 convert_element_type.32
  7.2 0.8 multiply_reduce_fusion
  8.1 1.4 multiply_convert_fusion.1
  9.5 0.0 all-gather.2.cloned.1.call-update
  9.5 0.0 reduce-scatter.2.cloned.1.call-start
  9.6 0.8 copy.20
  11.0 141.3 %all-gather.2.cloned.1.call-done = bf16[1,512,2048]{2,0,1:T(2,128)(2,1)} async-done(((bf16[1,4,2048]{2,0,1:T(2,128)(2,1)}), bf16[1,512,2048]{2,0,1:T(2,128)(2,1)}) %all-gather.2.cloned.1.call-update) | async-done | bytes 2097168 | tf_op jit(solution)/shard_map/all_gather | solution.py:47
  152.3 3.7 %constant_dynamic-slice_fusion.1 = bf16[1,256,2048]{2,0,1:T(2,128)(2,1)S(1)} fusion(bf16[1,512,2048]{2,0,1:T(2,128)(2,1)} %all-gather.2.cloned.1.call-done, s32[]{:T(128)S(6)} %select_n.15), kind=kLoop, calls=%fused_computation.11 | loop fusion | bytes 2097156 | tf_op jit(solution)/shard_map/dynamic_slice | solution.py:48
  156.1 0.6 copy.19
  156.7 1.3 pad.11
  158.0 138.4 %while.13 = (s32[]{:T(128)}, f32[2048,256]{1,0:T(8,128)S(1)}, s32[4]{0:T(128)S(1)}, bf16[4,2048]{1,0:T(4,128)(2,1)S(1)}, bf16[256,3328]{1,0:T(8,128)(2,1)}, /*in...) while((s32[]{:T(128)}, f32[2048,256]{1,0:T(8,128)S(1)}, ...), condition=%wide.region_2.3_spmd.clone, body=%wide.region_1.2_spmd.clone.sunk | while | flops 1074790400 | bytes 46711016 | solution.py:36
  158.0 0.6 dynamic_slice.38
  159.3 2.5 tile.16
  161.7 8.0 %reshape.39 = bf16[2099200]{0:T(1024)(128)(2,1)} reshape(bf16[4,512,1025]{2,1,0:T(8,128)(2,1)} %tile.16) | data formatting | bytes 8396800 | tf_op jit(solution)/shard_map/while
  169.7 5.7 %tile.17 = bf16[4,524800]{1,0:T(4,128)(2,1)} reshape(bf16[2099200]{0:T(1024)(128)(2,1)} %reshape.39) | data formatting | bytes 8396800 | tf_op jit(solution)/shard_map/while/body/eval_jaxpr/tile | solution.py:28
  175.4 5.3 %slice.9 = bf16[4,524288]{1,0:T(4,128)(2,1)} slice(bf16[4,524800]{1,0:T(4,128)(2,1)} %tile.17), slice={[0:4], [0:524288]} | slice | bytes 8388608 | tf_op jit(solution)/shard_map/while/body/eval_jaxpr/slice | solution.py:28
  180.7 8.0 %reshape.40 = bf16[2048,1024]{1,0:T(8,128)(2,1)} reshape(bf16[4,524288]{1,0:T(4,128)(2,1)} %slice.9) | data formatting | bytes 8388608 | tf_op jit(solution)/shard_map/while/body/eval_jaxpr/reshape | solution.py:28
  188.7 3.9 %convolution_add_fusion.2 = f32[2048,256]{1,0:T(8,128)S(1)} fusion(bf16[2048,1024]{1,0:T(8,128)(2,1)} %reshape.40, f32[2048,256]{1,0:T(8,128)S(1)} %get-tuple-element.142, pred[]{:T(512)S(6)} %compare.5, bf16[256,3328]{1,0:T(8,128)(2,1)} %get-tuple-element.156, s32[]{:T(128)S(6)} %select_n.21), kind=kOutput, calls=%fused_computation.clone.1 | convolution fusion | flops 1074790400 | bytes 8912901 | tf_op jit(solution)/shard_map/while/body/eval_jaxpr/dot_general | solution.py:30
  192.6 0.6 dynamic_slice.38
  193.9 2.5 tile.16
  196.3 8.0 %reshape.39 = bf16[2099200]{0:T(1024)(128)(2,1)} reshape(bf16[4,512,1025]{2,1,0:T(8,128)(2,1)} %tile.16) | data formatting | bytes 8396800 | tf_op jit(solution)/shard_map/while
  204.3 5.7 %tile.17 = bf16[4,524800]{1,0:T(4,128)(2,1)} reshape(bf16[2099200]{0:T(1024)(128)(2,1)} %reshape.39) | data formatting | bytes 8396800 | tf_op jit(solution)/shard_map/while/body/eval_jaxpr/tile | solution.py:28
  210.0 5.3 %slice.9 = bf16[4,524288]{1,0:T(4,128)(2,1)} slice(bf16[4,524800]{1,0:T(4,128)(2,1)} %tile.17), slice={[0:4], [0:524288]} | slice | bytes 8388608 | tf_op jit(solution)/shard_map/while/body/eval_jaxpr/slice | solution.py:28
  215.3 8.0 %reshape.40 = bf16[2048,1024]{1,0:T(8,128)(2,1)} reshape(bf16[4,524288]{1,0:T(4,128)(2,1)} %slice.9) | data formatting | bytes 8388608 | tf_op jit(solution)/shard_map/while/body/eval_jaxpr/reshape | solution.py:28
  223.3 3.9 %convolution_add_fusion.2 = f32[2048,256]{1,0:T(8,128)S(1)} fusion(bf16[2048,1024]{1,0:T(8,128)(2,1)} %reshape.40, f32[2048,256]{1,0:T(8,128)S(1)} %get-tuple-element.142, pred[]{:T(512)S(6)} %compare.5, bf16[256,3328]{1,0:T(8,128)(2,1)} %get-tuple-element.156, s32[]{:T(128)S(6)} %select_n.21), kind=kOutput, calls=%fused_computation.clone.1 | convolution fusion | flops 1074790400 | bytes 8912901 | tf_op jit(solution)/shard_map/while/body/eval_jaxpr/dot_general | solution.py:30
  227.2 0.6 dynamic_slice.38
  228.5 2.5 tile.16
  230.9 8.0 %reshape.39 = bf16[2099200]{0:T(1024)(128)(2,1)} reshape(bf16[4,512,1025]{2,1,0:T(8,128)(2,1)} %tile.16) | data formatting | bytes 8396800 | tf_op jit(solution)/shard_map/while
  238.9 5.7 %tile.17 = bf16[4,524800]{1,0:T(4,128)(2,1)} reshape(bf16[2099200]{0:T(1024)(128)(2,1)} %reshape.39) | data formatting | bytes 8396800 | tf_op jit(solution)/shard_map/while/body/eval_jaxpr/tile | solution.py:28
  244.6 5.3 %slice.9 = bf16[4,524288]{1,0:T(4,128)(2,1)} slice(bf16[4,524800]{1,0:T(4,128)(2,1)} %tile.17), slice={[0:4], [0:524288]} | slice | bytes 8388608 | tf_op jit(solution)/shard_map/while/body/eval_jaxpr/slice | solution.py:28
  249.9 8.0 %reshape.40 = bf16[2048,1024]{1,0:T(8,128)(2,1)} reshape(bf16[4,524288]{1,0:T(4,128)(2,1)} %slice.9) | data formatting | bytes 8388608 | tf_op jit(solution)/shard_map/while/body/eval_jaxpr/reshape | solution.py:28
  257.9 3.9 %convolution_add_fusion.2 = f32[2048,256]{1,0:T(8,128)S(1)} fusion(bf16[2048,1024]{1,0:T(8,128)(2,1)} %reshape.40, f32[2048,256]{1,0:T(8,128)S(1)} %get-tuple-element.142, pred[]{:T(512)S(6)} %compare.5, bf16[256,3328]{1,0:T(8,128)(2,1)} %get-tuple-element.156, s32[]{:T(128)S(6)} %select_n.21), kind=kOutput, calls=%fused_computation.clone.1 | convolution fusion | flops 1074790400 | bytes 8912901 | tf_op jit(solution)/shard_map/while/body/eval_jaxpr/dot_general | solution.py:30
  261.8 0.6 dynamic_slice.38
  263.1 2.5 tile.16
  265.5 8.0 %reshape.39 = bf16[2099200]{0:T(1024)(128)(2,1)} reshape(bf16[4,512,1025]{2,1,0:T(8,128)(2,1)} %tile.16) | data formatting | bytes 8396800 | tf_op jit(solution)/shard_map/while
  273.5 5.7 %tile.17 = bf16[4,524800]{1,0:T(4,128)(2,1)} reshape(bf16[2099200]{0:T(1024)(128)(2,1)} %reshape.39) | data formatting | bytes 8396800 | tf_op jit(solution)/shard_map/while/body/eval_jaxpr/tile | solution.py:28
  279.2 5.3 %slice.9 = bf16[4,524288]{1,0:T(4,128)(2,1)} slice(bf16[4,524800]{1,0:T(4,128)(2,1)} %tile.17), slice={[0:4], [0:524288]} | slice | bytes 8388608 | tf_op jit(solution)/shard_map/while/body/eval_jaxpr/slice | solution.py:28
  284.5 8.0 %reshape.40 = bf16[2048,1024]{1,0:T(8,128)(2,1)} reshape(bf16[4,524288]{1,0:T(4,128)(2,1)} %slice.9) | data formatting | bytes 8388608 | tf_op jit(solution)/shard_map/while/body/eval_jaxpr/reshape | solution.py:28
  292.5 3.9 %convolution_add_fusion.2 = f32[2048,256]{1,0:T(8,128)S(1)} fusion(bf16[2048,1024]{1,0:T(8,128)(2,1)} %reshape.40, f32[2048,256]{1,0:T(8,128)S(1)} %get-tuple-element.142, pred[]{:T(512)S(6)} %compare.5, bf16[256,3328]{1,0:T(8,128)(2,1)} %get-tuple-element.156, s32[]{:T(128)S(6)} %select_n.21), kind=kOutput, calls=%fused_computation.clone.1 | convolution fusion | flops 1074790400 | bytes 8912901 | tf_op jit(solution)/shard_map/while/body/eval_jaxpr/dot_general | solution.py:30
  296.4 1.1 convert_element_type.34
  297.5 0.0 reduce-scatter.2.cloned.1.call-update
  297.5 30.7 %reduce-scatter.2.cloned.1.call-done = bf16[128,4,256]{2,0,1:T(8,128)(2,1)} async-done(((bf16[512,4,256]{2,0,1:T(8,128)(2,1)}), bf16[128,4,256]{2,0,1:T(8,128)(2,1)}) %reduce-scatter.2.cloned.1.call-update) | async-done | bytes 262160 | tf_op jit(solution)/shard_map/reduce_scatter | solution.py:50
  328.2 1.0 multiply_convert_fusion
  329.2 0.9 copy.9
  (11 shorter events, 0.1 us)
Async XLA Ops:
  6.5 145.8 %all-gather.2.cloned.1.call-start = ((), (), s32[]{:S(2)}) async-start(), calls=%async_computation.1 | async-start | bytes 4227072 | tf_op jit(solution)/shard_map/all_gather | solution.py:47
  9.5 318.7 %reduce-scatter.2.cloned.1.call-start = ((), (), s32[]{:S(2)}) async-start(), calls=%async_computation.2 | async-start | bytes 1310720 | tf_op jit(solution)/shard_map/reduce_scatter | solution.py:50
Sparse Core Ops, SparseCore 0:
  11.9 140.3 all-gather.1
  297.6 30.5 reduce-scatter.1
where the time goes:
time: 338 us; the launch traced here: 337 us
  waiting for transfers between devices  172 us (51%)
  local copies, waits for them, and re-layouts  127 us (38%)
  matrix products  15.6 us (5%)
  between operations  14.1 us (4%)
  other arithmetic  5.03 us (1%)
    all_gather x1, waiting for transfers between devices, local(): gathered = lax.all_gather(normal, 'pairs', axis=1, tiled=True)  141 us
    another operation x8, local copies, waits for them, and re-layouts, one_block(): jnp.tile(extended, (1, count))[:, :count * width]  32.5 us
    reshape x4, local copies, waits for them, and re-layouts, one_block(): jnp.tile(extended, (1, count))[:, :count * width]  32 us
    while x4, local copies, waits for them, and re-layouts  31.9 us
    reduce_scatter x1, waiting for transfers between devices, local(): lax.psum_scatter(terms.astype(jnp.bfloat16), 'tm', scatter_dimension=0, t...  30.7 us
    slice x4, local copies, waits for them, and re-layouts, one_block(): jnp.tile(extended, (1, count))[:, :count * width]  21.2 us
    dot_general x4, matrix products, one_block(): lax.dot_general(skewed, window, (((1,), (1,)), ((), ())), preferred_eleme...  15.6 us
  transfers between devices with their start and end apart: 2, of which 2 were waited for; matrix products, arithmetic and copies ran while one was open for 0% of the time, Pallas kernels for 0%

commit v1 on v0

v1 whole, which is shorter than its diff:
```python
import jax
import jax.numpy as jnp
from jax import lax
from jax.experimental import pallas as pl
from jax.experimental.pallas import tpu as pltpu
from jax.sharding import Mesh, PartitionSpec as P

LAGS = 512
NBLK = 2
HALF = LAGS // 2
PAIR_AXES = ("x", "z", "yh", "core")
SIZES = {"x": 4, "z": 8, "yh": 2, "core": 2}
MiB = 1 << 20


def normalize_kernel(records_ref, alive_ref, out_ref):
    data = records_ref[0].astype(jnp.float32)
    power = jnp.mean(data * data, axis=-1, keepdims=True)
    scaled = data * lax.rsqrt(power + 1e-05) * alive_ref[...].astype(jnp.float32)
    out_ref[...] = scaled.astype(jnp.bfloat16)


def normalize(records, alive):
    _, rows, samples = records.shape
    return pl.pallas_call(
        normalize_kernel,
        out_shape=jax.ShapeDtypeStruct((rows, samples), jnp.bfloat16),
        in_specs=[pl.BlockSpec(memory_space=pltpu.VMEM)] * 2,
        out_specs=pl.BlockSpec(memory_space=pltpu.VMEM),
        name="normalize",
    )(records, alive.reshape(rows, 1))


def correlate_kernel(where_ref, own_ref, mine_ref, other_ref, *rest):
    outs, skew = rest[:-1], rest[-1]
    rows, samples = own_ref.shape
    chunk = outs[0].shape[1]
    width = skew.shape[2]
    half = samples // 2
    block, core, seg = where_ref[0], where_ref[1], where_ref[2]
    count = len(outs)
    for c in range(rows):
        line = own_ref[pl.ds(c, 1), :].astype(jnp.float32)
        line = jnp.concatenate(
            [jnp.zeros((1, chunk), jnp.float32), line, jnp.zeros((1, width - samples - chunk), jnp.float32)], axis=1
        )
        grid = jnp.broadcast_to(line, (chunk, width))
        skew[c] = pltpu.roll(grid, 0, 1, stride=1, stride_axis=0).astype(jnp.bfloat16)
    cols = mine_ref.shape[0] // NBLK
    first = pl.multiple_of(block * cols, cols)
    near = mine_ref[pl.ds(first, cols), :]
    far = other_ref[pl.ds(first, cols), :]
    for step in range(count):
        part = lax.rem(seg + 1 + step, count)
        start = chunk * (count - 1 - part)
        near_at = pl.multiple_of(start + core * half, chunk)
        far_at = pl.multiple_of(start + (1 - core) * half, chunk)
        for c in range(rows):
            total = lax.dot_general(
                skew[c, :, pl.ds(near_at, half)], near, (((1,), (1,)), ((), ())), preferred_element_type=jnp.float32
            )
            total += lax.dot_general(
                skew[c, :, pl.ds(far_at, half)], far, (((1,), (1,)), ((), ())), preferred_element_type=jnp.float32
            )
            outs[step][c] = total.astype(jnp.bfloat16)


def correlate(where, own, mine, other, segments):
    rows, samples = own.shape
    chunk = LAGS // segments
    width = samples + (LAGS - chunk)
    cols = mine.shape[0] // NBLK
    shape = jax.ShapeDtypeStruct((rows, chunk, cols), jnp.bfloat16)
    return pl.pallas_call(
        correlate_kernel,
        out_shape=[shape] * segments,
        in_specs=[pl.BlockSpec(memory_space=pltpu.SMEM)] + [pl.BlockSpec(memory_space=pltpu.VMEM)] * 3,
        out_specs=[pl.BlockSpec(memory_space=pltpu.VMEM)] * segments,
        scratch_shapes=[pltpu.VMEM((rows, chunk, width), jnp.bfloat16)],
        compiler_params=pltpu.CompilerParams(vmem_limit_bytes=40 * MiB),
        cost_estimate=pl.CostEstimate(
            flops=2 * rows * LAGS * samples * cols, bytes_accessed=4 * MiB, transcendentals=0
        ),
        name="correlate",
    )(where, own, mine, other)


def local(records, alive, tile_block):
    segments = lax.axis_size("tm")
    core, seg = lax.axis_index("core"), lax.axis_index("tm")
    normal = normalize(records, alive)
    rows, samples = normal.shape
    half = samples // 2
    chip = lax.all_gather(normal, ("yh", "core"), axis=0, tiled=True)
    share = lax.dynamic_slice_in_dim(chip, core * half, half, 1)
    peers = SIZES["x"] * SIZES["z"]
    sent = jnp.broadcast_to(share[None], (peers,) + share.shape)
    got = lax.all_to_all(sent, ("x", "z"), 0, 0, tiled=True)
    mine = got.reshape(peers * share.shape[0], half)
    other = lax.ppermute(mine, "core", [(0, 1), (1, 0)])
    where = jnp.stack([tile_block[0], core, seg]).astype(jnp.int32)
    parts = correlate(where, normal, mine, other, segments)
    total = parts[-1].astype(jnp.float32)
    for step in range(segments - 1):
        pairs = [(i, (i + 1 + step) % segments) for i in range(segments)]
        total = total + lax.ppermute(parts[step], "tm", pairs).astype(jnp.float32)
    return jnp.transpose((total / segments).astype(jnp.bfloat16), (1, 0, 2))


def solution(mesh):
    shape = tuple(SIZES[a] for a in PAIR_AXES) + (mesh.shape["tm"],)
    fine = Mesh(mesh.devices.reshape(shape), PAIR_AXES + ("tm",))
    in_specs = (P("tm", PAIR_AXES, None), P(PAIR_AXES), P(PAIR_AXES))
    out_specs = P("tm", PAIR_AXES, None)
    return jax.shard_map(local, mesh=fine, in_specs=in_specs, out_specs=out_specs, check_vma=False)
```

time: 338 us -> 96 us (0.28)
  the two profiles are of different devices: /device:TPU:1 before, /device:TPU:41 now
where the time goes in v1:
time: 96 us; the launch traced here: 95.6 us
  blocking collectives  47.8 us (50%)
  waiting for transfers between devices  21.3 us (22%)
  starting transfers between devices  15.1 us (16%)
  Pallas kernels  8.08 us (8%)
  local copies, waits for them, and re-layouts  2.4 us (2%)
    all_to_all x1, blocking collectives, local(): got = lax.all_to_all(sent, ('x', 'z'), 0, 0, tiled=True)  38 us
    ppermute x3, waiting for transfers between devices, local(): total = total + lax.ppermute(parts[step], 'tm', pairs).astype(jnp.float32)  19.7 us
    all_gather x1, blocking collectives, local(): chip = lax.all_gather(normal, ('yh', 'core'), axis=0, tiled=True)  9.85 us
    ppermute x3, starting transfers between devices, local(): total = total + lax.ppermute(parts[step], 'tm', pairs).astype(jnp.float32)  8.88 us
    pallas_call x1, Pallas kernels, correlate(): pl.pallas_call(correlate_kernel, out_shape=[shape] * segments, in_specs=[...  6.64 us
    ppermute x1, starting transfers between devices, local(): other = lax.ppermute(mine, 'core', [(0, 1), (1, 0)])  6.19 us
  transfers between devices with their start and end apart: 4, of which 4 were waited for; matrix products, arithmetic and copies ran while one was open for 0% of the time, Pallas kernels for 0%

profile of v1, /device:TPU:41, one launch (start us, length us, event | category | flops | bytes accessed | tf_op | source)
XLA Modules:
  0.0 95.6 jit_solution(11294527545225099708)
XLA Ops:
  0.0 0.0 copy-start.1
  0.0 0.7 copy-done.1
  0.7 0.7 copy.6.alive_ref
  1.3 1.4 %normalize.1.own_ref = bf16[4,2048]{1,0:T(4,128)(2,1)} custom-call(bf16[1,4,2048]{2,1,0:T(4,128)(2,1)} %records_ref.1, s32[4,1]{1,0:T(4,128)} %copy.6.alive_ref), custom_call_target="tpu_custom_call" | custom-call | tf_op jit(solution)/shard_map/normalize/pallas_call | solution.py:25
  2.8 9.9 %all-gather = bf16[4,4,2048]{2,1,0:T(4,128)(2,1)S(1)} all-gather(bf16[1,4,2048]{2,1,0:T(4,128)(2,1)} %bitcast.9), channel_id=1, replica_groups=mesh['x'=4,'z'=8,'yh'=2,'core'=2,'tm'=4] {'yh','core'}, dimensions={0}, use_global_device_ids=true | all-gather | bytes 81920 | tf_op jit(solution)/shard_map/all_gather | solution.py:94
  12.7 0.1 broadcast_in_dim.2
  12.8 0.0 copy-start
  12.8 38.0 %all_to_all.5 = bf16[32,16,1024]{2,1,0:T(8,128)(2,1)S(1)} all-to-all(bf16[32,16,1024]{2,1,0:T(8,128)(2,1)S(1)} %broadcast_in_dim.2), channel_id=1, replica_groups=mesh['x'=4,'z'=8,'yh'=2,'core'=2,'tm'=4] {'x','z'}, dimensions={0} | all-to-all | bytes 2097152 | tf_op jit(solution)/shard_map/all_to_all | solution.py:98
  50.8 6.2 %collective-permute-start = (bf16[512,1024]{1,0:T(8,128)(2,1)S(1)}, bf16[512,1024]{1,0:T(8,128)(2,1)S(1)}, u32[]{:S(2)}, u32[]{:S(2)}) collective-permute-start(bf16[512,1024]{1,0:T(8,128)(2,1)S(1)} %bitcast.7), channel_id=1, source_target_pairs={{0,4},{4,0},{1,5},{5,1},{2,6},{6,2},{3,7},{7,3},{8,12},{12,8},{9,1... | collective-permute-start | bytes 3145736 | tf_op jit(solution)/shard_map/ppermute | solution.py:100
  57.6 0.1 pad_add_fusion.where_ref
  57.7 1.5 %collective-permute-done.other_ref = bf16[512,1024]{1,0:T(8,128)(2,1)S(1)} collective-permute-done((bf16[512,1024]{1,0:T(8,128)(2,1)S(1)}, bf16[512,1024]{1,0:T(8,128)(2,1)S(1)}, u32[]{:S(2)}, u32[]{:S(2)}) %collective-permute-start) | collective-permute-done | bytes 1048608 | tf_op jit(solution)/shard_map/ppermute | solution.py:100
  59.2 0.0 copy-done
  59.2 6.6 %correlate.1 = (bf16[4,128,256]{2,1,0:T(8,128)(2,1)S(1)}, bf16[4,128,256]{2,1,0:T(8,128)(2,1)S(1)}, bf16[4,128,256]{2,1,0:T(8,128)(2,1)S(1)}, bf16[4,128,256]{2,1,0:T(8,128)(2,1)S(1)}) custom-call(s32[3]{0:T(128)S(1)} %pad_add_fusion.where_ref, bf16[4,2048]{1,0:T(4,128)(2,1)S(1)} %copy-done, bf16[512,1024]{1,0:T(8,128)(2,1)S(1)} %bitcast.8, ...), custom_call_target="tpu_custom_call" | custom-call | flops 2147483648 | bytes 4194304 | tf_op jit(solution)/shard_map/correlate/pallas_call | solution.py:74
  65.9 2.3 %collective-permute-start.1 = (bf16[4,128,256]{2,1,0:T(8,128)(2,1)S(1)}, bf16[4,128,256]{2,1,0:T(8,128)(2,1)S(1)}, u32[]{:S(2)}, u32[]{:S(2)}) collective-permute-start(bf16[4,128,256]{2,1,0:T(8,128)(2,1)S(1)} %get-tuple-element.10), channel_id=1, source_target_pairs={{0,1},{1,2},{2,3},{3,0},{4,5},{5,6},{6,7},{7,4},{8,9},{9,10},{10,1... | collective-permute-start | bytes 786440 | tf_op jit(solution)/shard_map/ppermute | solution.py:106
  68.2 4.7 %collective-permute-start.2 = (bf16[4,128,256]{2,1,0:T(8,128)(2,1)S(1)}, bf16[4,128,256]{2,1,0:T(8,128)(2,1)S(1)}, u32[]{:S(2)}, u32[]{:S(2)}) collective-permute-start(bf16[4,128,256]{2,1,0:T(8,128)(2,1)S(1)} %get-tuple-element.11), channel_id=1, source_target_pairs={{0,2},{1,3},{2,0},{3,1},{4,6},{5,7},{6,4},{7,5},{8,10},{9,11},{10,... | collective-permute-start | bytes 786440 | tf_op jit(solution)/shard_map/ppermute | solution.py:106
  72.8 1.9 %collective-permute-start.3 = (bf16[4,128,256]{2,1,0:T(8,128)(2,1)S(1)}, bf16[4,128,256]{2,1,0:T(8,128)(2,1)S(1)}, u32[]{:S(2)}, u32[]{:S(2)}) collective-permute-start(bf16[4,128,256]{2,1,0:T(8,128)(2,1)S(1)} %get-tuple-element.12), channel_id=1, source_target_pairs={{0,3},{1,0},{2,1},{3,2},{4,7},{5,4},{6,5},{7,6},{8,11},{9,8},{10,9... | collective-permute-start | bytes 786440 | tf_op jit(solution)/shard_map/ppermute | solution.py:106
  74.8 0.5 collective-permute-done.1
  75.3 15.0 %collective-permute-done.2 = bf16[4,128,256]{2,1,0:T(8,128)(2,1)S(1)} collective-permute-done((bf16[4,128,256]{2,1,0:T(8,128)(2,1)S(1)}, bf16[4,128,256]{2,1,0:T(8,128)(2,1)S(1)}, u32[]{:S(2)}, u32[]{:S(2)}) %collective-permute-start.2) | collective-permute-done | bytes 262176 | tf_op jit(solution)/shard_map/ppermute | solution.py:106
  90.3 4.2 %collective-permute-done.3 = bf16[4,128,256]{2,1,0:T(8,128)(2,1)S(1)} collective-permute-done((bf16[4,128,256]{2,1,0:T(8,128)(2,1)S(1)}, bf16[4,128,256]{2,1,0:T(8,128)(2,1)S(1)}, u32[]{:S(2)}, u32[]{:S(2)}) %collective-permute-start.3) | collective-permute-done | bytes 262176 | tf_op jit(solution)/shard_map/ppermute | solution.py:106
  94.5 0.2 fusion
  94.7 0.9 copy.7
  (2 shorter events, 0.0 us)
Async XLA Ops:
  0.0 0.7 copy-start.1
  12.8 46.4 %copy-start = (bf16[4,2048]{1,0:T(4,128)(2,1)S(1)}, bf16[4,2048]{1,0:T(4,128)(2,1)}, u32[]{:S(2)}) copy-start(bf16[4,2048]{1,0:T(4,128)(2,1)} %normalize.1.own_ref) | copy-start | bytes 49156
  50.8 8.5 %collective-permute-start = (bf16[512,1024]{1,0:T(8,128)(2,1)S(1)}, bf16[512,1024]{1,0:T(8,128)(2,1)S(1)}, u32[]{:S(2)}, u32[]{:S(2)}) collective-permute-start(bf16[512,1024]{1,0:T(8,128)(2,1)S(1)} %bitcast.7), channel_id=1, source_target_pairs={{0,4},{4,0},{1,5},{5,1},{2,6},{6,2},{3,7},{7,3},{8,12},{12,8},{9,1... | collective-permute-start | bytes 3145736 | tf_op jit(solution)/shard_map/ppermute | solution.py:100
  65.9 9.4 %collective-permute-start.1 = (bf16[4,128,256]{2,1,0:T(8,128)(2,1)S(1)}, bf16[4,128,256]{2,1,0:T(8,128)(2,1)S(1)}, u32[]{:S(2)}, u32[]{:S(2)}) collective-permute-start(bf16[4,128,256]{2,1,0:T(8,128)(2,1)S(1)} %get-tuple-element.10), channel_id=1, source_target_pairs={{0,1},{1,2},{2,3},{3,0},{4,5},{5,6},{6,7},{7,4},{8,9},{9,10},{10,1... | collective-permute-start | bytes 786440 | tf_op jit(solution)/shard_map/ppermute | solution.py:106
  68.2 22.2 %collective-permute-start.2 = (bf16[4,128,256]{2,1,0:T(8,128)(2,1)S(1)}, bf16[4,128,256]{2,1,0:T(8,128)(2,1)S(1)}, u32[]{:S(2)}, u32[]{:S(2)}) collective-permute-start(bf16[4,128,256]{2,1,0:T(8,128)(2,1)S(1)} %get-tuple-element.11), channel_id=1, source_target_pairs={{0,2},{1,3},{2,0},{3,1},{4,6},{5,7},{6,4},{7,5},{8,10},{9,11},{10,... | collective-permute-start | bytes 786440 | tf_op jit(solution)/shard_map/ppermute | solution.py:106
  72.8 21.7 %collective-permute-start.3 = (bf16[4,128,256]{2,1,0:T(8,128)(2,1)S(1)}, bf16[4,128,256]{2,1,0:T(8,128)(2,1)S(1)}, u32[]{:S(2)}, u32[]{:S(2)}) collective-permute-start(bf16[4,128,256]{2,1,0:T(8,128)(2,1)S(1)} %get-tuple-element.12), channel_id=1, source_target_pairs={{0,3},{1,0},{2,1},{3,2},{4,7},{5,4},{6,5},{7,6},{8,11},{9,8},{10,9... | collective-permute-start | bytes 786440 | tf_op jit(solution)/shard_map/ppermute | solution.py:106

commit v2 on v1

v2 whole, which is shorter than its diff:
```python
import jax
import jax.numpy as jnp
from jax import lax
from jax.experimental import pallas as pl
from jax.experimental.pallas import tpu as pltpu
from jax.sharding import Mesh, PartitionSpec as P

LAGS = 512
NBLK = 2
PAIR_AXES = ("x", "z", "yh", "core")
SIZES = {"x": 4, "z": 8, "yh": 2, "core": 2}
MiB = 1 << 20
SMEM = pl.BlockSpec(memory_space=pltpu.SMEM)
VMEM = pl.BlockSpec(memory_space=pltpu.VMEM)


def normalize_kernel(records_ref, alive_ref, out_ref):
    data = records_ref[0].astype(jnp.float32)
    power = jnp.mean(data * data, axis=-1, keepdims=True)
    row = lax.broadcasted_iota(jnp.int32, power.shape, 0)
    alive = jnp.zeros(power.shape, jnp.float32)
    for c in range(data.shape[0]):
        alive = jnp.where(row == c, alive_ref[c].astype(jnp.float32), alive)
    out_ref[...] = (data * lax.rsqrt(power + 1e-05) * alive).astype(jnp.bfloat16)


def normalize(records, alive):
    _, rows, samples = records.shape
    return pl.pallas_call(
        normalize_kernel,
        out_shape=jax.ShapeDtypeStruct((rows, samples), jnp.bfloat16),
        in_specs=[VMEM, SMEM],
        out_specs=VMEM,
        name="normalize",
    )(records, alive)


def correlate_kernel(rows, where_ref, own_ref, mine_ref, other_ref, *rest):
    out_refs, skew_ref = rest[:-1], rest[-1]
    samples, width = own_ref.shape[1], skew_ref.shape[1]
    chunk = skew_ref.shape[0] // rows
    cols, half = mine_ref.shape[0] // NBLK, mine_ref.shape[1]
    last = (width - samples) // chunk
    block, core = where_ref[0], where_ref[1]
    for c in range(rows):
        line = own_ref[pl.ds(c, 1), :].astype(jnp.float32)
        line = jnp.concatenate(
            [jnp.zeros((1, chunk), jnp.float32), line, jnp.zeros((1, width - samples - chunk), jnp.float32)], axis=1
        )
        grid = jnp.broadcast_to(line, (chunk, width))
        skewed = pltpu.roll(grid, 0, 1, stride=1, stride_axis=0)
        skew_ref[pl.ds(c * chunk, chunk), :] = skewed.astype(jnp.bfloat16)
    first = pl.multiple_of(block * cols, cols)
    for i, out_ref in enumerate(out_refs):
        start = chunk * (last - where_ref[2 + i])
        total = 0.0
        for at, ref in ((core, mine_ref), (1 - core, other_ref)):
            window = pl.ds(pl.multiple_of(start + at * half, chunk), half)
            total += lax.dot_general(
                skew_ref[:, window], ref[pl.ds(first, cols), :], (((1,), (1,)), ((), ())),
                preferred_element_type=jnp.float32,
            )
        out_ref[...] = total.astype(jnp.bfloat16).reshape(out_ref.shape)


def correlate(where, own, mine, other):
    rows, samples = own.shape
    count = where.shape[0] - 2
    chunk = LAGS // count
    width = samples + LAGS - chunk
    cols = mine.shape[0] // NBLK
    shape = jax.ShapeDtypeStruct((rows, chunk, cols), jnp.bfloat16)
    return pl.pallas_call(
        lambda *refs: correlate_kernel(rows, *refs),
        out_shape=[shape] * count,
        in_specs=[SMEM, VMEM, VMEM, VMEM],
        out_specs=[VMEM] * count,
        scratch_shapes=[pltpu.VMEM((rows * chunk, width), jnp.bfloat16)],
        compiler_params=pltpu.CompilerParams(vmem_limit_bytes=40 * MiB),
        cost_estimate=pl.CostEstimate(
            flops=2 * rows * LAGS * samples * cols, bytes_accessed=4 * MiB, transcendentals=0
        ),
        name="correlate",
    )(where, own, mine, other)


def local(records, alive, tile_block):
    segments = lax.axis_size("tm")
    core, seg = lax.axis_index("core"), lax.axis_index("tm")
    normal = normalize(records, alive)
    rows, samples = normal.shape
    half = samples // 2
    chip = lax.all_gather(normal, "core", axis=0, tiled=True)
    share = lax.dynamic_slice_in_dim(chip, core * half, half, 1)
    for axes in (("z", "yh"), ("x",)):
        peers = 1
        for axis in axes:
            peers *= SIZES[axis]
        sent = jnp.broadcast_to(share[None], (peers,) + share.shape)
        share = lax.all_to_all(sent, axes, 0, 0, tiled=True).reshape(peers * share.shape[0], half)
    other = lax.ppermute(share, "core", [(0, 1), (1, 0)])
    shifts = (2, 1, 3, 0)
    owners = [lax.rem(seg + shift, segments) for shift in shifts]
    where = jnp.stack([tile_block[0], core] + owners).astype(jnp.int32)
    terms = correlate(where, normal, share, other)
    total = terms[-1].astype(jnp.float32)
    for shift, term in zip(shifts[:-1], terms):
        term = lax.ppermute(term, "tm", [(i, (i + shift) % segments) for i in range(segments)])
        total = total + term.astype(jnp.float32)
    return jnp.transpose((total / segments).astype(jnp.bfloat16), (1, 0, 2))


def solution(mesh):
    shape = tuple(SIZES[a] for a in PAIR_AXES) + (mesh.shape["tm"],)
    fine = Mesh(mesh.devices.reshape(shape), PAIR_AXES + ("tm",))
    in_specs = (P("tm", PAIR_AXES, None), P(PAIR_AXES), P(PAIR_AXES))
    out_specs = P("tm", PAIR_AXES, None)
    return jax.shard_map(local, mesh=fine, in_specs=in_specs, out_specs=out_specs, check_vma=False)
```

time: 96 us -> 87.6 us (0.912)
  the two profiles are of different devices: /device:TPU:41 before, /device:TPU:8 now
where the time goes in v2:
time: 87.6 us; the launch traced here: 87.3 us
  blocking collectives  51.5 us (59%)
  waiting for transfers between devices  19 us (22%)
  starting transfers between devices  9.67 us (11%)
  Pallas kernels  4.99 us (6%)
  local copies, waits for them, and re-layouts  1.16 us (1%)
    all_to_all x2, blocking collectives, local(): lax.all_to_all(sent, axes, 0, 0, tiled=True)  49.5 us
    ppermute x3, waiting for transfers between devices, local(): lax.ppermute(term, 'tm', [(i, (i + shift) % segments) for i in range(segm...  17.2 us
    ppermute x3, starting transfers between devices, local(): lax.ppermute(term, 'tm', [(i, (i + shift) % segments) for i in range(segm...  7.76 us
    pallas_call x1, Pallas kernels, correlate(): pl.pallas_call(lambda *refs: correlate_kernel(rows, *refs), out_shape=[sh...  3.48 us
    all_gather x1, blocking collectives, local(): chip = lax.all_gather(normal, 'core', axis=0, tiled=True)  2.03 us
    ppermute x1, starting transfers between devices, local(): other = lax.ppermute(share, 'core', [(0, 1), (1, 0)])  1.91 us
    ppermute x1, waiting for transfers between devices, local(): other = lax.ppermute(share, 'core', [(0, 1), (1, 0)])  1.87 us
  transfers between devices with their start and end apart: 4, of which 4 were waited for; matrix products, arithmetic and copies ran while one was open for 0% of the time, Pallas kernels for 0%

profile of v2, /device:TPU:8, one launch (start us, length us, event | category | flops | bytes accessed | tf_op | source)
XLA Modules:
  0.0 87.3 jit_solution(3368434416416737407)
XLA Ops:
  0.0 1.5 %normalize.1.refs_1_ = bf16[4,2048]{1,0:T(4,128)(2,1)} custom-call(bf16[1,4,2048]{2,1,0:T(4,128)(2,1)} %records_ref.1, s32[4]{0:T(128)} %alive_ref.1), custom_call_target="tpu_custom_call" | custom-call | tf_op jit(solution)/shard_map/normalize/pallas_call | solution.py:29
  1.5 2.0 %all-gather = bf16[2,4,2048]{2,1,0:T(4,128)(2,1)S(1)} all-gather(bf16[1,4,2048]{2,1,0:T(4,128)(2,1)} %bitcast.12), channel_id=1, replica_groups=mesh['x'=4,'z'=8,'yh'=2,'core'=2,'tm'=4] {'core'}, dimensions={0}, use_global_device_ids=true | all-gather | bytes 49152 | tf_op jit(solution)/shard_map/all_gather | solution.py:93
  3.6 31.1 %all_to_all.10 = bf16[16,8,1024]{2,1,0:T(8,128)(2,1)S(1)} all-to-all(bf16[16,8,1024]{2,1,0:T(8,128)(2,1)S(1)} %broadcast_in_dim.6), channel_id=1, replica_groups=mesh['x'=4,'z'=8,'yh'=2,'core'=2,'tm'=4] {'z','yh'}, dimensions={0} | all-to-all | bytes 524288 | tf_op jit(solution)/shard_map/all_to_all | solution.py:100
  34.8 0.1 broadcast_in_dim.15
  34.9 18.3 %all_to_all.11 = bf16[4,128,1024]{2,1,0:T(8,128)(2,1)S(1)} all-to-all(bf16[4,128,1024]{2,1,0:T(8,128)(2,1)S(1)} %broadcast_in_dim.15), channel_id=1, replica_groups=mesh['x'=4,'z'=8,'yh'=2,'core'=2,'tm'=4] {'x'}, dimensions={0} | all-to-all | bytes 2097152 | tf_op jit(solution)/shard_map/all_to_all | solution.py:100
  53.2 1.9 %collective-permute-start = (bf16[512,1024]{1,0:T(8,128)(2,1)S(1)}, bf16[512,1024]{1,0:T(8,128)(2,1)S(1)}, u32[]{:S(2)}, u32[]{:S(2)}) collective-permute-start(bf16[512,1024]{1,0:T(8,128)(2,1)S(1)} %bitcast.10), channel_id=1, source_target_pairs={{0,4},{4,0},{1,5},{5,1},{2,6},{6,2},{3,7},{7,3},{8,12},{12,8},{9,1... | collective-permute-start | bytes 3145736 | tf_op jit(solution)/shard_map/ppermute | solution.py:101
  55.1 0.0 copy-start
  55.8 0.1 stack.23.refs_0_
  55.9 1.9 %collective-permute-done.refs_3_ = bf16[512,1024]{1,0:T(8,128)(2,1)S(1)} collective-permute-done((bf16[512,1024]{1,0:T(8,128)(2,1)S(1)}, bf16[512,1024]{1,0:T(8,128)(2,1)S(1)}, u32[]{:S(2)}, u32[]{:S(2)}) %collective-permute-start) | collective-permute-done | bytes 1048608 | tf_op jit(solution)/shard_map/ppermute | solution.py:101
  57.8 0.0 copy-done
  57.8 3.5 %correlate.1 = (bf16[4,128,256]{2,1,0:T(8,128)(2,1)S(1)}, bf16[4,128,256]{2,1,0:T(8,128)(2,1)S(1)}, bf16[4,128,256]{2,1,0:T(8,128)(2,1)S(1)}, bf16[4,128,256]{2,1,0:T(8,128)(2,1)S(1)}) custom-call(s32[6]{0:T(128)S(1)} %stack.23.refs_0_, bf16[4,2048]{1,0:T(4,128)(2,1)S(1)} %copy-done, bf16[512,1024]{1,0:T(8,128)(2,1)S(1)} %bitcast.11, ...), custom_call_target="tpu_custom_call" | custom-call | flops 2147483648 | bytes 4194304 | tf_op jit(solution)/shard_map/correlate/pallas_call | solution.py:73
  61.2 1.9 %collective-permute-start.1 = (bf16[4,128,256]{2,1,0:T(8,128)(2,1)S(1)}, bf16[4,128,256]{2,1,0:T(8,128)(2,1)S(1)}, u32[]{:S(2)}, u32[]{:S(2)}) collective-permute-start(bf16[4,128,256]{2,1,0:T(8,128)(2,1)S(1)} %get-tuple-element.10), channel_id=1, source_target_pairs={{0,2},{1,3},{2,0},{3,1},{4,6},{5,7},{6,4},{7,5},{8,10},{9,11},{10,... | collective-permute-start | bytes 786440 | tf_op jit(solution)/shard_map/ppermute | solution.py:108
  63.2 1.9 %collective-permute-start.2 = (bf16[4,128,256]{2,1,0:T(8,128)(2,1)S(1)}, bf16[4,128,256]{2,1,0:T(8,128)(2,1)S(1)}, u32[]{:S(2)}, u32[]{:S(2)}) collective-permute-start(bf16[4,128,256]{2,1,0:T(8,128)(2,1)S(1)} %get-tuple-element.11), channel_id=1, source_target_pairs={{0,1},{1,2},{2,3},{3,0},{4,5},{5,6},{6,7},{7,4},{8,9},{9,10},{10,1... | collective-permute-start | bytes 786440 | tf_op jit(solution)/shard_map/ppermute | solution.py:108
  65.1 3.9 %collective-permute-start.3 = (bf16[4,128,256]{2,1,0:T(8,128)(2,1)S(1)}, bf16[4,128,256]{2,1,0:T(8,128)(2,1)S(1)}, u32[]{:S(2)}, u32[]{:S(2)}) collective-permute-start(bf16[4,128,256]{2,1,0:T(8,128)(2,1)S(1)} %get-tuple-element.12), channel_id=1, source_target_pairs={{0,3},{1,0},{2,1},{3,2},{4,7},{5,4},{6,5},{7,6},{8,11},{9,8},{10,9... | collective-permute-start | bytes 786440 | tf_op jit(solution)/shard_map/ppermute | solution.py:108
  69.0 4.4 %collective-permute-done.1 = bf16[4,128,256]{2,1,0:T(8,128)(2,1)S(1)} collective-permute-done((bf16[4,128,256]{2,1,0:T(8,128)(2,1)S(1)}, bf16[4,128,256]{2,1,0:T(8,128)(2,1)S(1)}, u32[]{:S(2)}, u32[]{:S(2)}) %collective-permute-start.1) | collective-permute-done | bytes 262176 | tf_op jit(solution)/shard_map/ppermute | solution.py:108
  73.4 10.9 %collective-permute-done.2 = bf16[4,128,256]{2,1,0:T(8,128)(2,1)S(1)} collective-permute-done((bf16[4,128,256]{2,1,0:T(8,128)(2,1)S(1)}, bf16[4,128,256]{2,1,0:T(8,128)(2,1)S(1)}, u32[]{:S(2)}, u32[]{:S(2)}) %collective-permute-start.2) | collective-permute-done | bytes 262176 | tf_op jit(solution)/shard_map/ppermute | solution.py:108
  84.3 1.9 %collective-permute-done.3 = bf16[4,128,256]{2,1,0:T(8,128)(2,1)S(1)} collective-permute-done((bf16[4,128,256]{2,1,0:T(8,128)(2,1)S(1)}, bf16[4,128,256]{2,1,0:T(8,128)(2,1)S(1)}, u32[]{:S(2)}, u32[]{:S(2)}) %collective-permute-start.3) | collective-permute-done | bytes 262176 | tf_op jit(solution)/shard_map/ppermute | solution.py:108
  86.2 0.2 fusion
  86.4 0.9 %copy.5 = bf16[128,4,256]{2,1,0:T(4,128)(2,1)} copy(bf16[128,4,256]{2,0,1:T(8,128)(2,1)S(1)} %fusion) | data formatting | bytes 524288 | tf_op jit(solution)/shard_map/transpose | solution.py:110
  (3 shorter events, 0.0 us)
Async XLA Ops:
  53.2 4.5 %collective-permute-start = (bf16[512,1024]{1,0:T(8,128)(2,1)S(1)}, bf16[512,1024]{1,0:T(8,128)(2,1)S(1)}, u32[]{:S(2)}, u32[]{:S(2)}) collective-permute-start(bf16[512,1024]{1,0:T(8,128)(2,1)S(1)} %bitcast.10), channel_id=1, source_target_pairs={{0,4},{4,0},{1,5},{5,1},{2,6},{6,2},{3,7},{7,3},{8,12},{12,8},{9,1... | collective-permute-start | bytes 3145736 | tf_op jit(solution)/shard_map/ppermute | solution.py:101
  55.1 2.6 %copy-start = (bf16[4,2048]{1,0:T(4,128)(2,1)S(1)}, bf16[4,2048]{1,0:T(4,128)(2,1)}, u32[]{:S(2)}) copy-start(bf16[4,2048]{1,0:T(4,128)(2,1)} %normalize.1.refs_1_) | copy-start | bytes 49156
  61.2 12.2 %collective-permute-start.1 = (bf16[4,128,256]{2,1,0:T(8,128)(2,1)S(1)}, bf16[4,128,256]{2,1,0:T(8,128)(2,1)S(1)}, u32[]{:S(2)}, u32[]{:S(2)}) collective-permute-start(bf16[4,128,256]{2,1,0:T(8,128)(2,1)S(1)} %get-tuple-element.10), channel_id=1, source_target_pairs={{0,2},{1,3},{2,0},{3,1},{4,6},{5,7},{6,4},{7,5},{8,10},{9,11},{10,... | collective-permute-start | bytes 786440 | tf_op jit(solution)/shard_map/ppermute | solution.py:108
  63.2 21.1 %collective-permute-start.2 = (bf16[4,128,256]{2,1,0:T(8,128)(2,1)S(1)}, bf16[4,128,256]{2,1,0:T(8,128)(2,1)S(1)}, u32[]{:S(2)}, u32[]{:S(2)}) collective-permute-start(bf16[4,128,256]{2,1,0:T(8,128)(2,1)S(1)} %get-tuple-element.11), channel_id=1, source_target_pairs={{0,1},{1,2},{2,3},{3,0},{4,5},{5,6},{6,7},{7,4},{8,9},{9,10},{10,1... | collective-permute-start | bytes 786440 | tf_op jit(solution)/shard_map/ppermute | solution.py:108
  65.1 21.1 %collective-permute-start.3 = (bf16[4,128,256]{2,1,0:T(8,128)(2,1)S(1)}, bf16[4,128,256]{2,1,0:T(8,128)(2,1)S(1)}, u32[]{:S(2)}, u32[]{:S(2)}) collective-permute-start(bf16[4,128,256]{2,1,0:T(8,128)(2,1)S(1)} %get-tuple-element.12), channel_id=1, source_target_pairs={{0,3},{1,0},{2,1},{3,2},{4,7},{5,4},{6,5},{7,6},{8,11},{9,8},{10,9... | collective-permute-start | bytes 786440 | tf_op jit(solution)/shard_map/ppermute | solution.py:108

commit v3 on v2

v3 whole, which is shorter than its diff:
```python
import jax
import jax.numpy as jnp
from jax import lax
from jax.experimental import pallas as pl
from jax.experimental.pallas import tpu as pltpu
from jax.sharding import Mesh, PartitionSpec as P

LAGS = 512
NBLK = 2
PAIR_AXES = ("x", "z", "yh", "core")
SIZES = {"x": 4, "z": 8, "yh": 2, "core": 2}
MiB = 1 << 20
SMEM = pl.BlockSpec(memory_space=pltpu.SMEM)
VMEM = pl.BlockSpec(memory_space=pltpu.VMEM)


def normalize_kernel(records_ref, alive_ref, out_ref, copies_ref):
    data = records_ref[0].astype(jnp.float32)
    power = jnp.mean(data * data, axis=-1, keepdims=True)
    row = lax.broadcasted_iota(jnp.int32, power.shape, 0)
    alive = jnp.zeros(power.shape, jnp.float32)
    for c in range(data.shape[0]):
        alive = jnp.where(row == c, alive_ref[c].astype(jnp.float32), alive)
    normal = (data * lax.rsqrt(power + 1e-05) * alive).astype(jnp.bfloat16)
    out_ref[...] = normal
    for i in range(copies_ref.shape[0]):
        copies_ref[i] = normal


def normalize(records, alive, copies):
    _, rows, samples = records.shape
    return pl.pallas_call(
        normalize_kernel,
        out_shape=[
            jax.ShapeDtypeStruct((rows, samples), jnp.bfloat16),
            jax.ShapeDtypeStruct((copies, rows, samples), jnp.bfloat16),
        ],
        in_specs=[VMEM, SMEM],
        out_specs=[VMEM, VMEM],
        name="normalize",
    )(records, alive)


def correlate_kernel(rows, where_ref, own_ref, mine_ref, other_ref, *rest):
    out_refs, skew_ref, cols_ref = rest[:-2], rest[-2], rest[-1]
    samples, width = own_ref.shape[1], skew_ref.shape[1]
    chunk = skew_ref.shape[0] // rows
    cols = cols_ref.shape[0]
    half = cols // 2
    last = (width - samples) // chunk
    block, core = where_ref[0], where_ref[1]
    for c in range(rows):
        line = own_ref[pl.ds(c, 1), :].astype(jnp.float32)
        line = jnp.concatenate(
            [jnp.zeros((1, chunk), jnp.float32), line, jnp.zeros((1, width - samples - chunk), jnp.float32)], axis=1
        )
        grid = jnp.broadcast_to(line, (chunk, width))
        skewed = pltpu.roll(grid, 0, 1, stride=1, stride_axis=0)
        skew_ref[pl.ds(c * chunk, chunk), :] = skewed.astype(jnp.bfloat16)
    first = block * half
    group = 2 * rows
    upper = lax.broadcasted_iota(jnp.int32, (group, samples), 0) < rows
    for at in range(0, half, 2 * group):
        here = pl.ds(pl.multiple_of(first + at, 2 * group), 2 * group)
        near, far = mine_ref[here, :].astype(jnp.float32), other_ref[here, :].astype(jnp.float32)
        even, odd = jnp.where(core == 0, near, far), jnp.where(core == 0, far, near)
        woven = []
        for part in range(2):
            e, o = even[part * group : (part + 1) * group], odd[part * group : (part + 1) * group]
            woven += [jnp.where(upper, e, pltpu.roll(o, rows, 0)), jnp.where(upper, pltpu.roll(e, rows, 0), o)]
        cols_ref[pl.ds(2 * at, 4 * group), :] = jnp.concatenate(woven, axis=0).astype(jnp.bfloat16)
    for i, out_ref in enumerate(out_refs):
        window = pl.ds(pl.multiple_of(chunk * (last - where_ref[2 + i]), chunk), samples)
        total = lax.dot_general(
            skew_ref[:, window], cols_ref[...], (((1,), (1,)), ((), ())), preferred_element_type=jnp.float32
        )
        out_ref[...] = total.astype(jnp.bfloat16).reshape(out_ref.shape)


def correlate(where, own, mine, other):
    rows, samples = own.shape
    count = where.shape[0] - 2
    chunk = LAGS // count
    width = samples + LAGS - chunk
    cols = 2 * mine.shape[0] // NBLK
    shape = jax.ShapeDtypeStruct((rows, chunk, cols), jnp.bfloat16)
    return pl.pallas_call(
        lambda *refs: correlate_kernel(rows, *refs),
        out_shape=[shape] * count,
        in_specs=[SMEM, VMEM, VMEM, VMEM],
        out_specs=[VMEM] * count,
        scratch_shapes=[pltpu.VMEM((rows * chunk, width), jnp.bfloat16), pltpu.VMEM((cols, samples), jnp.bfloat16)],
        compiler_params=pltpu.CompilerParams(vmem_limit_bytes=40 * MiB),
        cost_estimate=pl.CostEstimate(
            flops=2 * rows * LAGS * samples * cols, bytes_accessed=4 * MiB, transcendentals=0
        ),
        name="correlate",
    )(where, own, mine, other)


def local(records, alive, tile_block):
    segments = lax.axis_size("tm")
    core, seg = lax.axis_index("core"), lax.axis_index("tm")
    normal, sent = normalize(records, alive, SIZES["z"] * SIZES["yh"])
    slab = lax.all_to_all(sent, ("z", "yh"), 0, 0, tiled=True).reshape(-1, sent.shape[2])
    sent = jnp.broadcast_to(slab[None], (SIZES["x"],) + slab.shape)
    share = lax.all_to_all(sent, "x", 0, 0, tiled=True).reshape(-1, slab.shape[1])
    other = lax.ppermute(share, "core", [(0, 1), (1, 0)])
    shifts = (2, 1, 3, 0)
    owners = [lax.rem(seg + shift, segments) for shift in shifts]
    where = jnp.stack([tile_block[0], core] + owners).astype(jnp.int32)
    terms = correlate(where, normal, share, other)
    total = terms[-1].astype(jnp.float32)
    for shift, term in zip(shifts[:-1], terms):
        term = lax.ppermute(term, "tm", [(i, (i + shift) % segments) for i in range(segments)])
        total = total + term.astype(jnp.float32)
    return jnp.transpose((total / segments).astype(jnp.bfloat16), (1, 0, 2))


def solution(mesh):
    shape = tuple(SIZES[a] for a in PAIR_AXES) + (mesh.shape["tm"],)
    fine = Mesh(mesh.devices.reshape(shape), PAIR_AXES + ("tm",))
    in_specs = (P("tm", PAIR_AXES, None), P(PAIR_AXES), P(PAIR_AXES))
    out_specs = P("tm", PAIR_AXES, None)
    return jax.shard_map(local, mesh=fine, in_specs=in_specs, out_specs=out_specs, check_vma=False)
```

time: 87.6 us -> 85.9 us (0.981)
  blocking collectives: 51.5 us -> 49.3 us
    all_gather x1 -> x0, blocking collectives: 2.03 us -> none  [local(): chip = lax.all_gather(normal, 'core', axis=0, tiled=True)]
where the time goes in v3:
time: 85.9 us; the launch traced here: 85.4 us
  blocking collectives  49.3 us (57%)
  waiting for transfers between devices  19.2 us (22%)
  starting transfers between devices  9.67 us (11%)
  Pallas kernels  5.13 us (6%)
  local copies, waits for them, and re-layouts  1.17 us (1%)
    all_to_all x1, blocking collectives, local(): lax.all_to_all(sent, ('z', 'yh'), 0, 0, tiled=True)  31 us
    all_to_all x1, blocking collectives, local(): lax.all_to_all(sent, 'x', 0, 0, tiled=True).reshape(-1, slab.shape[1])  18.3 us
    ppermute x3, waiting for transfers between devices, local(): lax.ppermute(term, 'tm', [(i, (i + shift) % segments) for i in range(segm...  17.3 us
    ppermute x3, starting transfers between devices, local(): lax.ppermute(term, 'tm', [(i, (i + shift) % segments) for i in range(segm...  7.76 us
    pallas_call x1, Pallas kernels, correlate(): pl.pallas_call(lambda *refs: correlate_kernel(rows, *refs), out_shape=[sh...  3.5 us
    ppermute x1, starting transfers between devices, local(): other = lax.ppermute(share, 'core', [(0, 1), (1, 0)])  1.91 us
    ppermute x1, waiting for transfers between devices, local(): other = lax.ppermute(share, 'core', [(0, 1), (1, 0)])  1.87 us
  transfers between devices with their start and end apart: 4, of which 4 were waited for; matrix products, arithmetic and copies ran while one was open for 0% of the time, Pallas kernels for 0%

profile of v3, /device:TPU:8, one launch (start us, length us, event | category | flops | bytes accessed | tf_op | source)
XLA Modules:
  0.0 85.4 jit_solution(10126778872517268345)
XLA Ops:
  0.0 1.6 %normalize.1 = (bf16[4,2048]{1,0:T(4,128)(2,1)}, bf16[16,4,2048]{2,1,0:T(4,128)(2,1)}) custom-call(bf16[1,4,2048]{2,1,0:T(4,128)(2,1)} %records_ref.1, s32[4]{0:T(128)} %alive_ref.1), custom_call_target="tpu_custom_call" | custom-call | tf_op jit(solution)/shard_map/normalize/pallas_call | solution.py:32
  1.6 31.0 %all_to_all.10 = bf16[16,4,2048]{2,1,0:T(4,128)(2,1)S(1)} all-to-all(bf16[16,4,2048]{2,1,0:T(4,128)(2,1)} %get-tuple-element.12), channel_id=1, replica_groups=mesh['x'=4,'z'=8,'yh'=2,'core'=2,'tm'=4] {'z','yh'}, dimensions={0} | all-to-all | bytes 524288 | tf_op jit(solution)/shard_map/all_to_all | solution.py:105
  32.6 0.1 broadcast_in_dim.7
  32.7 0.1 broadcast_in_dim.8
  32.8 18.3 %all_to_all.11 = bf16[4,64,2048]{2,1,0:T(8,128)(2,1)S(1)} all-to-all(bf16[4,64,2048]{2,1,0:T(8,128)(2,1)S(1)} %broadcast_in_dim.8), channel_id=1, replica_groups=mesh['x'=4,'z'=8,'yh'=2,'core'=2,'tm'=4] {'x'}, dimensions={0} | all-to-all | bytes 2097152 | tf_op jit(solution)/shard_map/all_to_all | solution.py:107
  51.2 1.9 %collective-permute-start = (bf16[256,2048]{1,0:T(8,128)(2,1)S(1)}, bf16[256,2048]{1,0:T(8,128)(2,1)S(1)}, u32[]{:S(2)}, u32[]{:S(2)}) collective-permute-start(bf16[256,2048]{1,0:T(8,128)(2,1)S(1)} %bitcast.8), channel_id=1, source_target_pairs={{0,4},{4,0},{1,5},{5,1},{2,6},{6,2},{3,7},{7,3},{8,12},{12,8},{9,1... | collective-permute-start | bytes 3145736 | tf_op jit(solution)/shard_map/ppermute | solution.py:108
  53.1 0.0 copy-start
  53.8 0.1 stack.23.refs_0_
  53.8 1.9 %collective-permute-done.refs_3_ = bf16[256,2048]{1,0:T(8,128)(2,1)S(1)} collective-permute-done((bf16[256,2048]{1,0:T(8,128)(2,1)S(1)}, bf16[256,2048]{1,0:T(8,128)(2,1)S(1)}, u32[]{:S(2)}, u32[]{:S(2)}) %collective-permute-start) | collective-permute-done | bytes 1048608 | tf_op jit(solution)/shard_map/ppermute | solution.py:108
  55.7 0.0 copy-done
  55.7 3.5 %correlate.1 = (bf16[4,128,256]{2,1,0:T(8,128)(2,1)S(1)}, bf16[4,128,256]{2,1,0:T(8,128)(2,1)S(1)}, bf16[4,128,256]{2,1,0:T(8,128)(2,1)S(1)}, bf16[4,128,256]{2,1,0:T(8,128)(2,1)S(1)}) custom-call(s32[6]{0:T(128)S(1)} %stack.23.refs_0_, bf16[4,2048]{1,0:T(4,128)(2,1)S(1)} %copy-done, bf16[256,2048]{1,0:T(8,128)(2,1)S(1)} %bitcast.9, ...), custom_call_target="tpu_custom_call" | custom-call | flops 2147483648 | bytes 4194304 | tf_op jit(solution)/shard_map/correlate/pallas_call | solution.py:87
  59.2 1.9 %collective-permute-start.1 = (bf16[4,128,256]{2,1,0:T(8,128)(2,1)S(1)}, bf16[4,128,256]{2,1,0:T(8,128)(2,1)S(1)}, u32[]{:S(2)}, u32[]{:S(2)}) collective-permute-start(bf16[4,128,256]{2,1,0:T(8,128)(2,1)S(1)} %get-tuple-element.14), channel_id=1, source_target_pairs={{0,2},{1,3},{2,0},{3,1},{4,6},{5,7},{6,4},{7,5},{8,10},{9,11},{10,... | collective-permute-start | bytes 786440 | tf_op jit(solution)/shard_map/ppermute | solution.py:115
  61.1 1.9 %collective-permute-start.2 = (bf16[4,128,256]{2,1,0:T(8,128)(2,1)S(1)}, bf16[4,128,256]{2,1,0:T(8,128)(2,1)S(1)}, u32[]{:S(2)}, u32[]{:S(2)}) collective-permute-start(bf16[4,128,256]{2,1,0:T(8,128)(2,1)S(1)} %get-tuple-element.15), channel_id=1, source_target_pairs={{0,1},{1,2},{2,3},{3,0},{4,5},{5,6},{6,7},{7,4},{8,9},{9,10},{10,1... | collective-permute-start | bytes 786440 | tf_op jit(solution)/shard_map/ppermute | solution.py:115
  63.1 3.9 %collective-permute-start.3 = (bf16[4,128,256]{2,1,0:T(8,128)(2,1)S(1)}, bf16[4,128,256]{2,1,0:T(8,128)(2,1)S(1)}, u32[]{:S(2)}, u32[]{:S(2)}) collective-permute-start(bf16[4,128,256]{2,1,0:T(8,128)(2,1)S(1)} %get-tuple-element.16), channel_id=1, source_target_pairs={{0,3},{1,0},{2,1},{3,2},{4,7},{5,4},{6,5},{7,6},{8,11},{9,8},{10,9... | collective-permute-start | bytes 786440 | tf_op jit(solution)/shard_map/ppermute | solution.py:115
  67.0 4.7 %collective-permute-done.1 = bf16[4,128,256]{2,1,0:T(8,128)(2,1)S(1)} collective-permute-done((bf16[4,128,256]{2,1,0:T(8,128)(2,1)S(1)}, bf16[4,128,256]{2,1,0:T(8,128)(2,1)S(1)}, u32[]{:S(2)}, u32[]{:S(2)}) %collective-permute-start.1) | collective-permute-done | bytes 262176 | tf_op jit(solution)/shard_map/ppermute | solution.py:115
  71.7 10.7 %collective-permute-done.2 = bf16[4,128,256]{2,1,0:T(8,128)(2,1)S(1)} collective-permute-done((bf16[4,128,256]{2,1,0:T(8,128)(2,1)S(1)}, bf16[4,128,256]{2,1,0:T(8,128)(2,1)S(1)}, u32[]{:S(2)}, u32[]{:S(2)}) %collective-permute-start.2) | collective-permute-done | bytes 262176 | tf_op jit(solution)/shard_map/ppermute | solution.py:115
  82.4 2.0 %collective-permute-done.3 = bf16[4,128,256]{2,1,0:T(8,128)(2,1)S(1)} collective-permute-done((bf16[4,128,256]{2,1,0:T(8,128)(2,1)S(1)}, bf16[4,128,256]{2,1,0:T(8,128)(2,1)S(1)}, u32[]{:S(2)}, u32[]{:S(2)}) %collective-permute-start.3) | collective-permute-done | bytes 262176 | tf_op jit(solution)/shard_map/ppermute | solution.py:115
  84.4 0.2 fusion
  84.5 0.9 %copy.4 = bf16[128,4,256]{2,1,0:T(4,128)(2,1)} copy(bf16[128,4,256]{2,0,1:T(8,128)(2,1)S(1)} %fusion) | data formatting | bytes 524288 | tf_op jit(solution)/shard_map/transpose | solution.py:117
Async XLA Ops:
  51.2 4.5 %collective-permute-start = (bf16[256,2048]{1,0:T(8,128)(2,1)S(1)}, bf16[256,2048]{1,0:T(8,128)(2,1)S(1)}, u32[]{:S(2)}, u32[]{:S(2)}) collective-permute-start(bf16[256,2048]{1,0:T(8,128)(2,1)S(1)} %bitcast.8), channel_id=1, source_target_pairs={{0,4},{4,0},{1,5},{5,1},{2,6},{6,2},{3,7},{7,3},{8,12},{12,8},{9,1... | collective-permute-start | bytes 3145736 | tf_op jit(solution)/shard_map/ppermute | solution.py:108
  53.1 2.6 %copy-start = (bf16[4,2048]{1,0:T(4,128)(2,1)S(1)}, bf16[4,2048]{1,0:T(4,128)(2,1)}, u32[]{:S(2)}) copy-start(bf16[4,2048]{1,0:T(4,128)(2,1)} %get-tuple-element.11.refs_1_) | copy-start | bytes 49156
  59.2 12.5 %collective-permute-start.1 = (bf16[4,128,256]{2,1,0:T(8,128)(2,1)S(1)}, bf16[4,128,256]{2,1,0:T(8,128)(2,1)S(1)}, u32[]{:S(2)}, u32[]{:S(2)}) collective-permute-start(bf16[4,128,256]{2,1,0:T(8,128)(2,1)S(1)} %get-tuple-element.14), channel_id=1, source_target_pairs={{0,2},{1,3},{2,0},{3,1},{4,6},{5,7},{6,4},{7,5},{8,10},{9,11},{10,... | collective-permute-start | bytes 786440 | tf_op jit(solution)/shard_map/ppermute | solution.py:115
  61.1 21.2 %collective-permute-start.2 = (bf16[4,128,256]{2,1,0:T(8,128)(2,1)S(1)}, bf16[4,128,256]{2,1,0:T(8,128)(2,1)S(1)}, u32[]{:S(2)}, u32[]{:S(2)}) collective-permute-start(bf16[4,128,256]{2,1,0:T(8,128)(2,1)S(1)} %get-tuple-element.15), channel_id=1, source_target_pairs={{0,1},{1,2},{2,3},{3,0},{4,5},{5,6},{6,7},{7,4},{8,9},{9,10},{10,1... | collective-permute-start | bytes 786440 | tf_op jit(solution)/shard_map/ppermute | solution.py:115
  63.1 21.3 %collective-permute-start.3 = (bf16[4,128,256]{2,1,0:T(8,128)(2,1)S(1)}, bf16[4,128,256]{2,1,0:T(8,128)(2,1)S(1)}, u32[]{:S(2)}, u32[]{:S(2)}) collective-permute-start(bf16[4,128,256]{2,1,0:T(8,128)(2,1)S(1)} %get-tuple-element.16), channel_id=1, source_target_pairs={{0,3},{1,0},{2,1},{3,2},{4,7},{5,4},{6,5},{7,6},{8,11},{9,8},{10,9... | collective-permute-start | bytes 786440 | tf_op jit(solution)/shard_map/ppermute | solution.py:115

commit v4 on v3

--- a/solution.py
+++ b/solution.py
@@ -10,6 +10,7 @@
 PAIR_AXES = ("x", "z", "yh", "core")
 SIZES = {"x": 4, "z": 8, "yh": 2, "core": 2}
 MiB = 1 << 20
+SENDS = ((3, 2, 1, 0), (2, 0, 3, 1), (1, 3, 0, 2), (0, 1, 2, 3))
 SMEM = pl.BlockSpec(memory_space=pltpu.SMEM)
 VMEM = pl.BlockSpec(memory_space=pltpu.VMEM)
 
@@ -106,14 +107,23 @@
     sent = jnp.broadcast_to(slab[None], (SIZES["x"],) + slab.shape)
     share = lax.all_to_all(sent, "x", 0, 0, tiled=True).reshape(-1, slab.shape[1])
     other = lax.ppermute(share, "core", [(0, 1), (1, 0)])
-    shifts = (2, 1, 3, 0)
-    owners = [lax.rem(seg + shift, segments) for shift in shifts]
-    where = jnp.stack([tile_block[0], core] + owners).astype(jnp.int32)
-    terms = correlate(where, normal, share, other)
-    total = terms[-1].astype(jnp.float32)
-    for shift, term in zip(shifts[:-1], terms):
-        term = lax.ppermute(term, "tm", [(i, (i + shift) % segments) for i in range(segments)])
-        total = total + term.astype(jnp.float32)
+    sends = []
+    for column in zip(*SENDS):
+        value = column[-1]
+        for i in reversed(range(segments - 1)):
+            value = jnp.where(seg == i, column[i], value)
+        sends.append(value)
+    where = jnp.stack([tile_block[0], core] + sends).astype(jnp.int32)
+    near, turned, later, own = correlate(where, normal, share, other)
+    inner = (seg == 1) | (seg == 2)
+    turned = lax.ppermute(turned, "tm", [(0, 2), (3, 1), (1, 0), (2, 3)])
+    passed = lax.ppermute(near, "tm", [(0, 1), (3, 2)])
+    passed = jnp.where(inner, passed.astype(jnp.float32), 0.0)
+    middle = lax.ppermute(near, "tm", [(1, 2), (2, 1)])
+    later = (later.astype(jnp.float32) + passed).astype(jnp.bfloat16)
+    last = lax.ppermute(later, "tm", [(0, 1), (3, 2), (1, 3), (2, 0)])
+    total = own.astype(jnp.float32) + turned.astype(jnp.float32) + last.astype(jnp.float32)
+    total = total + jnp.where(inner, middle.astype(jnp.float32), 0.0)
     return jnp.transpose((total / segments).astype(jnp.bfloat16), (1, 0, 2))
 
 

time: 85.9 us -> 84.9 us (0.988)
  the two profiles are of different devices: /device:TPU:8 before, /device:TPU:1 now
where the time goes in v4:
time: 84.9 us; the launch traced here: 84.4 us
  blocking collectives  45.7 us (54%)
  starting transfers between devices  18.8 us (22%)
  waiting for transfers between devices  12.6 us (15%)
  Pallas kernels  5.13 us (6%)
  local copies, waits for them, and re-layouts  1.17 us (1%)
    all_to_all x1, blocking collectives, local(): lax.all_to_all(sent, ('z', 'yh'), 0, 0, tiled=True)  29.1 us
    all_to_all x1, blocking collectives, local(): lax.all_to_all(sent, 'x', 0, 0, tiled=True).reshape(-1, slab.shape[1])  16.6 us
    ppermute x1, waiting for transfers between devices, local(): last = lax.ppermute(later, 'tm', [(0, 1), (3, 2), (1, 3), (2, 0)])  8.79 us
    ppermute x1, starting transfers between devices, local(): other = lax.ppermute(share, 'core', [(0, 1), (1, 0)])  5.17 us
    ppermute x1, starting transfers between devices, local(): passed = lax.ppermute(near, 'tm', [(0, 1), (3, 2)])  5.13 us
    ppermute x1, starting transfers between devices, local(): last = lax.ppermute(later, 'tm', [(0, 1), (3, 2), (1, 3), (2, 0)])  4.11 us
    ppermute x1, starting transfers between devices, local(): turned = lax.ppermute(turned, 'tm', [(0, 2), (3, 1), (1, 0), (2, 3)])  3.69 us
    pallas_call x1, Pallas kernels, correlate(): pl.pallas_call(lambda *refs: correlate_kernel(rows, *refs), out_shape=[sh...  3.5 us
  transfers between devices with their start and end apart: 5, of which 4 were waited for; matrix products, arithmetic and copies ran while one was open for 0% of the time, Pallas kernels for 0%

profile of v4, /device:TPU:1, one launch (start us, length us, event | category | flops | bytes accessed | tf_op | source)
XLA Modules:
  0.0 84.4 jit_solution(12671522946673482091)
XLA Ops:
  0.0 1.6 %normalize.1 = (bf16[4,2048]{1,0:T(4,128)(2,1)}, bf16[16,4,2048]{2,1,0:T(4,128)(2,1)}) custom-call(bf16[1,4,2048]{2,1,0:T(4,128)(2,1)} %records_ref.1, s32[4]{0:T(128)} %alive_ref.1), custom_call_target="tpu_custom_call" | custom-call | tf_op jit(solution)/shard_map/normalize/pallas_call | solution.py:33
  1.6 29.1 %all_to_all.10 = bf16[16,4,2048]{2,1,0:T(4,128)(2,1)S(1)} all-to-all(bf16[16,4,2048]{2,1,0:T(4,128)(2,1)} %get-tuple-element.12), channel_id=1, replica_groups=mesh['x'=4,'z'=8,'yh'=2,'core'=2,'tm'=4] {'z','yh'}, dimensions={0} | all-to-all | bytes 524288 | tf_op jit(solution)/shard_map/all_to_all | solution.py:106
  30.7 0.1 broadcast_in_dim.12
  30.8 0.1 broadcast_in_dim.13
  30.9 16.6 %all_to_all.11 = bf16[4,64,2048]{2,1,0:T(8,128)(2,1)S(1)} all-to-all(bf16[4,64,2048]{2,1,0:T(8,128)(2,1)S(1)} %broadcast_in_dim.13), channel_id=1, replica_groups=mesh['x'=4,'z'=8,'yh'=2,'core'=2,'tm'=4] {'x'}, dimensions={0} | all-to-all | bytes 2097152 | tf_op jit(solution)/shard_map/all_to_all | solution.py:108
  47.5 5.2 %collective-permute-start = (bf16[256,2048]{1,0:T(8,128)(2,1)S(1)}, bf16[256,2048]{1,0:T(8,128)(2,1)S(1)}, u32[]{:S(2)}, u32[]{:S(2)}) collective-permute-start(bf16[256,2048]{1,0:T(8,128)(2,1)S(1)} %bitcast.8), channel_id=1, source_target_pairs={{0,4},{4,0},{1,5},{5,1},{2,6},{6,2},{3,7},{7,3},{8,12},{12,8},{9,1... | collective-permute-start | bytes 3145736 | tf_op jit(solution)/shard_map/ppermute | solution.py:109
  52.7 0.0 copy-start
  53.4 0.1 stack.23.refs_0_
  53.5 1.5 %collective-permute-done.refs_3_ = bf16[256,2048]{1,0:T(8,128)(2,1)S(1)} collective-permute-done((bf16[256,2048]{1,0:T(8,128)(2,1)S(1)}, bf16[256,2048]{1,0:T(8,128)(2,1)S(1)}, u32[]{:S(2)}, u32[]{:S(2)}) %collective-permute-start) | collective-permute-done | bytes 1048608 | tf_op jit(solution)/shard_map/ppermute | solution.py:109
  54.9 0.0 copy-done
  54.9 3.5 %correlate.1 = (bf16[4,128,256]{2,1,0:T(8,128)(2,1)S(1)}, bf16[4,128,256]{2,1,0:T(8,128)(2,1)S(1)}, bf16[4,128,256]{2,1,0:T(8,128)(2,1)S(1)}, bf16[4,128,256]{2,1,0:T(8,128)(2,1)S(1)}) custom-call(s32[6]{0:T(128)S(1)} %stack.23.refs_0_, bf16[4,2048]{1,0:T(4,128)(2,1)S(1)} %copy-done, bf16[256,2048]{1,0:T(8,128)(2,1)S(1)} %bitcast.9, ...), custom_call_target="tpu_custom_call" | custom-call | flops 2147483648 | bytes 4194304 | tf_op jit(solution)/shard_map/correlate/pallas_call | solution.py:88
  58.5 5.1 %collective-permute-start.2 = (bf16[4,128,256]{2,1,0:T(8,128)(2,1)S(1)}, bf16[4,128,256]{2,1,0:T(8,128)(2,1)S(1)}, u32[]{:S(2)}, u32[]{:S(2)}) collective-permute-start(bf16[4,128,256]{2,1,0:T(8,128)(2,1)S(1)} %get-tuple-element.16), channel_id=1, source_target_pairs={{0,1},{3,2},{4,5},{7,6},{8,9},{11,10},{12,13},{15,14},{16,17},{19,... | collective-permute-start | bytes 786440 | tf_op jit(solution)/shard_map/ppermute | solution.py:120
  63.6 0.7 collective-permute-start.4
  64.3 3.7 %collective-permute-start.1 = (bf16[4,128,256]{2,1,0:T(8,128)(2,1)S(1)}, bf16[4,128,256]{2,1,0:T(8,128)(2,1)S(1)}, u32[]{:S(2)}, u32[]{:S(2)}) collective-permute-start(bf16[4,128,256]{2,1,0:T(8,128)(2,1)S(1)} %get-tuple-element.14), channel_id=1, source_target_pairs={{0,2},{3,1},{1,0},{2,3},{4,6},{7,5},{5,4},{6,7},{8,10},{11,9},{9,8... | collective-permute-start | bytes 786440 | tf_op jit(solution)/shard_map/ppermute | solution.py:119
  68.0 0.9 %collective-permute-done.2 = bf16[4,128,256]{2,1,0:T(8,128)(2,1)S(1)} collective-permute-done((bf16[4,128,256]{2,1,0:T(8,128)(2,1)S(1)}, bf16[4,128,256]{2,1,0:T(8,128)(2,1)S(1)}, u32[]{:S(2)}, u32[]{:S(2)}) %collective-permute-start.2) | collective-permute-done | bytes 262176 | tf_op jit(solution)/shard_map/ppermute | solution.py:120
  68.9 0.1 add_convert_fusion
  69.0 4.1 %collective-permute-start.3 = (bf16[4,128,256]{2,1,0:T(8,128)(2,1)S(1)}, bf16[4,128,256]{2,1,0:T(8,128)(2,1)S(1)}, u32[]{:S(2)}, u32[]{:S(2)}) collective-permute-start(bf16[4,128,256]{2,1,0:T(8,128)(2,1)S(1)} %add_convert_fusion), channel_id=1, source_target_pairs={{0,1},{3,2},{1,3},{2,0},{4,5},{7,6},{5,7},{6,4},{8,9},{11,10},{9,1... | collective-permute-start | bytes 786440 | tf_op jit(solution)/shard_map/ppermute | solution.py:124
  73.1 1.5 %collective-permute-done.1 = bf16[4,128,256]{2,1,0:T(8,128)(2,1)S(1)} collective-permute-done((bf16[4,128,256]{2,1,0:T(8,128)(2,1)S(1)}, bf16[4,128,256]{2,1,0:T(8,128)(2,1)S(1)}, u32[]{:S(2)}, u32[]{:S(2)}) %collective-permute-start.1) | collective-permute-done | bytes 262176 | tf_op jit(solution)/shard_map/ppermute | solution.py:119
  74.5 0.0 collective-permute-done.4
  74.5 8.8 %collective-permute-done.3 = bf16[4,128,256]{2,1,0:T(8,128)(2,1)S(1)} collective-permute-done((bf16[4,128,256]{2,1,0:T(8,128)(2,1)S(1)}, bf16[4,128,256]{2,1,0:T(8,128)(2,1)S(1)}, u32[]{:S(2)}, u32[]{:S(2)}) %collective-permute-start.3) | collective-permute-done | bytes 262176 | tf_op jit(solution)/shard_map/ppermute | solution.py:124
  83.3 0.2 fusion
  83.5 0.9 %copy.4 = bf16[128,4,256]{2,1,0:T(4,128)(2,1)} copy(bf16[128,4,256]{2,0,1:T(8,128)(2,1)S(1)} %fusion) | data formatting | bytes 524288 | tf_op jit(solution)/shard_map/transpose | solution.py:127
Async XLA Ops:
  47.5 7.4 %collective-permute-start = (bf16[256,2048]{1,0:T(8,128)(2,1)S(1)}, bf16[256,2048]{1,0:T(8,128)(2,1)S(1)}, u32[]{:S(2)}, u32[]{:S(2)}) collective-permute-start(bf16[256,2048]{1,0:T(8,128)(2,1)S(1)} %bitcast.8), channel_id=1, source_target_pairs={{0,4},{4,0},{1,5},{5,1},{2,6},{6,2},{3,7},{7,3},{8,12},{12,8},{9,1... | collective-permute-start | bytes 3145736 | tf_op jit(solution)/shard_map/ppermute | solution.py:109
  52.7 2.2 %copy-start = (bf16[4,2048]{1,0:T(4,128)(2,1)S(1)}, bf16[4,2048]{1,0:T(4,128)(2,1)}, u32[]{:S(2)}) copy-start(bf16[4,2048]{1,0:T(4,128)(2,1)} %get-tuple-element.11.refs_1_) | copy-start | bytes 49156
  58.5 10.4 %collective-permute-start.2 = (bf16[4,128,256]{2,1,0:T(8,128)(2,1)S(1)}, bf16[4,128,256]{2,1,0:T(8,128)(2,1)S(1)}, u32[]{:S(2)}, u32[]{:S(2)}) collective-permute-start(bf16[4,128,256]{2,1,0:T(8,128)(2,1)S(1)} %get-tuple-element.16), channel_id=1, source_target_pairs={{0,1},{3,2},{4,5},{7,6},{8,9},{11,10},{12,13},{15,14},{16,17},{19,... | collective-permute-start | bytes 786440 | tf_op jit(solution)/shard_map/ppermute | solution.py:120
  63.6 10.9 %collective-permute-start.4 = (bf16[4,128,256]{2,1,0:T(8,128)(2,1)S(1)}, bf16[4,128,256]{2,1,0:T(8,128)(2,1)S(1)}, u32[]{:S(2)}, u32[]{:S(2)}) collective-permute-start(bf16[4,128,256]{2,1,0:T(8,128)(2,1)S(1)} %get-tuple-element.16), channel_id=1, source_target_pairs={{1,2},{2,1},{5,6},{6,5},{9,10},{10,9},{13,14},{14,13},{17,18},{18,... | collective-permute-start | bytes 786440 | tf_op jit(solution)/shard_map/ppermute | solution.py:122
  64.3 10.3 %collective-permute-start.1 = (bf16[4,128,256]{2,1,0:T(8,128)(2,1)S(1)}, bf16[4,128,256]{2,1,0:T(8,128)(2,1)S(1)}, u32[]{:S(2)}, u32[]{:S(2)}) collective-permute-start(bf16[4,128,256]{2,1,0:T(8,128)(2,1)S(1)} %get-tuple-element.14), channel_id=1, source_target_pairs={{0,2},{3,1},{1,0},{2,3},{4,6},{7,5},{5,4},{6,7},{8,10},{11,9},{9,8... | collective-permute-start | bytes 786440 | tf_op jit(solution)/shard_map/ppermute | solution.py:119
  69.0 14.4 %collective-permute-start.3 = (bf16[4,128,256]{2,1,0:T(8,128)(2,1)S(1)}, bf16[4,128,256]{2,1,0:T(8,128)(2,1)S(1)}, u32[]{:S(2)}, u32[]{:S(2)}) collective-permute-start(bf16[4,128,256]{2,1,0:T(8,128)(2,1)S(1)} %add_convert_fusion), channel_id=1, source_target_pairs={{0,1},{3,2},{1,3},{2,0},{4,5},{7,6},{5,7},{6,4},{8,9},{11,10},{9,1... | collective-permute-start | bytes 786440 | tf_op jit(solution)/shard_map/ppermute | solution.py:124

commit v5 on v4

--- a/solution.py
+++ b/solution.py
@@ -78,10 +78,10 @@
         out_ref[...] = total.astype(jnp.bfloat16).reshape(out_ref.shape)
 
 
-def correlate(where, own, mine, other):
+def correlate(where, segments, own, mine, other):
     rows, samples = own.shape
     count = where.shape[0] - 2
-    chunk = LAGS // count
+    chunk = LAGS // segments
     width = samples + LAGS - chunk
     cols = 2 * mine.shape[0] // NBLK
     shape = jax.ShapeDtypeStruct((rows, chunk, cols), jnp.bfloat16)
@@ -93,7 +93,7 @@
         scratch_shapes=[pltpu.VMEM((rows * chunk, width), jnp.bfloat16), pltpu.VMEM((cols, samples), jnp.bfloat16)],
         compiler_params=pltpu.CompilerParams(vmem_limit_bytes=40 * MiB),
         cost_estimate=pl.CostEstimate(
-            flops=2 * rows * LAGS * samples * cols, bytes_accessed=4 * MiB, transcendentals=0
+            flops=2 * rows * count * chunk * samples * cols, bytes_accessed=4 * MiB, transcendentals=0
         ),
         name="correlate",
     )(where, own, mine, other)
@@ -113,8 +113,10 @@
         for i in reversed(range(segments - 1)):
             value = jnp.where(seg == i, column[i], value)
         sends.append(value)
-    where = jnp.stack([tile_block[0], core] + sends).astype(jnp.int32)
-    near, turned, later, own = correlate(where, normal, share, other)
+    early = jnp.stack([tile_block[0], core] + sends[:2]).astype(jnp.int32)
+    late = jnp.stack([tile_block[0], core] + sends[2:]).astype(jnp.int32)
+    near, turned = correlate(early, segments, normal, share, other)
+    later, own = correlate(late, segments, normal, share, other)
     inner = (seg == 1) | (seg == 2)
     turned = lax.ppermute(turned, "tm", [(0, 2), (3, 1), (1, 0), (2, 3)])
     passed = lax.ppermute(near, "tm", [(0, 1), (3, 2)])

time: 84.9 us -> 83.9 us (0.988)
  starting transfers between devices: 18.8 us -> 17.1 us
  Pallas kernels: 5.13 us -> 6.47 us
    ppermute x1, starting transfers between devices: 4.11 us -> 2.46 us  [local(): last = lax.ppermute(later, 'tm', [(0, 1), (3, 2), (1, 3), (2, 0)])]
    pallas_call x1 -> x2, Pallas kernels: 3.5 us -> 4.85 us  [correlate(): pl.pallas_call(lambda *refs: correlate_kernel(rows, *refs), out_shape=[sh...]
    ppermute x1, waiting for transfers between devices: 0.89 us -> 0.01 us  [local(): passed = lax.ppermute(near, 'tm', [(0, 1), (3, 2)])]
  transfers between devices with their start and end apart: 5 -> 5, of which waited for: 4 -> 3; matrix products, arithmetic and copies ran while one was open for 0% -> 0% of each run, Pallas kernels for 0% -> 3%
where the time goes in v5:
time: 83.9 us; the launch traced here: 83.4 us
  blocking collectives  45.7 us (54%)
  starting transfers between devices  17.1 us (20%)
  waiting for transfers between devices  11.8 us (14%)
  Pallas kernels  6.47 us (8%)
  local copies, waits for them, and re-layouts  1.09 us (1%)
    all_to_all x1, blocking collectives, local(): lax.all_to_all(sent, ('z', 'yh'), 0, 0, tiled=True)  29.1 us
    all_to_all x1, blocking collectives, local(): lax.all_to_all(sent, 'x', 0, 0, tiled=True).reshape(-1, slab.shape[1])  16.6 us
    ppermute x1, waiting for transfers between devices, local(): last = lax.ppermute(later, 'tm', [(0, 1), (3, 2), (1, 3), (2, 0)])  8.88 us
    ppermute x1, starting transfers between devices, local(): other = lax.ppermute(share, 'core', [(0, 1), (1, 0)])  5.17 us
    ppermute x1, starting transfers between devices, local(): passed = lax.ppermute(near, 'tm', [(0, 1), (3, 2)])  5.13 us
    pallas_call x2, Pallas kernels, correlate(): pl.pallas_call(lambda *refs: correlate_kernel(rows, *refs), out_shape=[sh...  4.85 us
    ppermute x1, starting transfers between devices, local(): turned = lax.ppermute(turned, 'tm', [(0, 2), (3, 1), (1, 0), (2, 3)])  3.69 us
    ppermute x1, starting transfers between devices, local(): last = lax.ppermute(later, 'tm', [(0, 1), (3, 2), (1, 3), (2, 0)])  2.46 us
  transfers between devices with their start and end apart: 5, of which 3 were waited for; matrix products, arithmetic and copies ran while one was open for 0% of the time, Pallas kernels for 3%

profile of v5, /device:TPU:1, one launch (start us, length us, event | category | flops | bytes accessed | tf_op | source)
XLA Modules:
  0.0 83.4 jit_solution(15625956439170670554)
XLA Ops:
  0.0 1.6 %normalize.1 = (bf16[4,2048]{1,0:T(4,128)(2,1)}, bf16[16,4,2048]{2,1,0:T(4,128)(2,1)}) custom-call(bf16[1,4,2048]{2,1,0:T(4,128)(2,1)} %records_ref.1, s32[4]{0:T(128)} %alive_ref.1), custom_call_target="tpu_custom_call" | custom-call | tf_op jit(solution)/shard_map/normalize/pallas_call | solution.py:33
  1.6 29.1 %all_to_all.10 = bf16[16,4,2048]{2,1,0:T(4,128)(2,1)S(1)} all-to-all(bf16[16,4,2048]{2,1,0:T(4,128)(2,1)} %get-tuple-element.12), channel_id=1, replica_groups=mesh['x'=4,'z'=8,'yh'=2,'core'=2,'tm'=4] {'z','yh'}, dimensions={0} | all-to-all | bytes 524288 | tf_op jit(solution)/shard_map/all_to_all | solution.py:106
  30.7 0.1 broadcast_in_dim.12
  30.8 0.1 broadcast_in_dim.13
  30.9 16.6 %all_to_all.11 = bf16[4,64,2048]{2,1,0:T(8,128)(2,1)S(1)} all-to-all(bf16[4,64,2048]{2,1,0:T(8,128)(2,1)S(1)} %broadcast_in_dim.13), channel_id=1, replica_groups=mesh['x'=4,'z'=8,'yh'=2,'core'=2,'tm'=4] {'x'}, dimensions={0} | all-to-all | bytes 2097152 | tf_op jit(solution)/shard_map/all_to_all | solution.py:108
  47.5 5.2 %collective-permute-start = (bf16[256,2048]{1,0:T(8,128)(2,1)S(1)}, bf16[256,2048]{1,0:T(8,128)(2,1)S(1)}, u32[]{:S(2)}, u32[]{:S(2)}) collective-permute-start(bf16[256,2048]{1,0:T(8,128)(2,1)S(1)} %bitcast.8), channel_id=1, source_target_pairs={{0,4},{4,0},{1,5},{5,1},{2,6},{6,2},{3,7},{7,3},{8,12},{12,8},{9,1... | collective-permute-start | bytes 3145736 | tf_op jit(solution)/shard_map/ppermute | solution.py:109
  52.7 0.0 copy-start
  53.4 0.1 pad_add_fusion.2.refs_0_
  53.4 1.5 %collective-permute-done.refs_3_ = bf16[256,2048]{1,0:T(8,128)(2,1)S(1)} collective-permute-done((bf16[256,2048]{1,0:T(8,128)(2,1)S(1)}, bf16[256,2048]{1,0:T(8,128)(2,1)S(1)}, u32[]{:S(2)}, u32[]{:S(2)}) %collective-permute-start) | collective-permute-done | bytes 1048608 | tf_op jit(solution)/shard_map/ppermute | solution.py:109
  54.9 0.0 copy-done
  54.9 2.4 %correlate.3 = (bf16[4,128,256]{2,1,0:T(8,128)(2,1)S(1)}, bf16[4,128,256]{2,1,0:T(8,128)(2,1)S(1)}) custom-call(s32[4]{0:T(128)S(1)} %pad_add_fusion.2.refs_0_, bf16[4,2048]{1,0:T(4,128)(2,1)S(1)} %copy-done, bf16[256,2048]{1,0:T(8,128)(2,1)S(1)} %bitcast.9, bf16[256,2048]{1,0:T(8,128)(2,1)S(1)} %collective-permute-done.refs_3_), custom_call_target="tpu_custom_call" | custom-call | flops 1073741824 | bytes 4194304 | tf_op jit(solution)/shard_map/correlate/pallas_call | solution.py:88
  57.4 5.1 %collective-permute-start.2 = (bf16[4,128,256]{2,1,0:T(8,128)(2,1)S(1)}, bf16[4,128,256]{2,1,0:T(8,128)(2,1)S(1)}, u32[]{:S(2)}, u32[]{:S(2)}) collective-permute-start(bf16[4,128,256]{2,1,0:T(8,128)(2,1)S(1)} %get-tuple-element.16), channel_id=1, source_target_pairs={{0,1},{3,2},{4,5},{7,6},{8,9},{11,10},{12,13},{15,14},{16,17},{19,... | collective-permute-start | bytes 786440 | tf_op jit(solution)/shard_map/ppermute | solution.py:122
  62.5 0.1 pad_add_fusion.refs_0_
  62.6 0.7 collective-permute-start.4
  63.3 3.7 %collective-permute-start.1 = (bf16[4,128,256]{2,1,0:T(8,128)(2,1)S(1)}, bf16[4,128,256]{2,1,0:T(8,128)(2,1)S(1)}, u32[]{:S(2)}, u32[]{:S(2)}) collective-permute-start(bf16[4,128,256]{2,1,0:T(8,128)(2,1)S(1)} %get-tuple-element.14), channel_id=1, source_target_pairs={{0,2},{3,1},{1,0},{2,3},{4,6},{7,5},{5,4},{6,7},{8,10},{11,9},{9,8... | collective-permute-start | bytes 786440 | tf_op jit(solution)/shard_map/ppermute | solution.py:121
  67.0 2.4 %correlate.2 = (bf16[4,128,256]{2,1,0:T(8,128)(2,1)S(1)}, bf16[4,128,256]{2,1,0:T(8,128)(2,1)S(1)}) custom-call(s32[4]{0:T(128)S(1)} %pad_add_fusion.refs_0_, bf16[4,2048]{1,0:T(4,128)(2,1)S(1)} %copy-done, bf16[256,2048]{1,0:T(8,128)(2,1)S(1)} %bitcast.10, bf16[256,2048]{1,0:T(8,128)(2,1)S(1)} %collective-permute-done.refs_3_), custom_call_target="tpu_custom_call" | custom-call | flops 1073741824 | bytes 4194304 | tf_op jit(solution)/shard_map/correlate/pallas_call | solution.py:88
  69.4 0.0 collective-permute-done.2
  69.4 0.1 add_convert_fusion
  69.5 2.5 %collective-permute-start.3 = (bf16[4,128,256]{2,1,0:T(8,128)(2,1)S(1)}, bf16[4,128,256]{2,1,0:T(8,128)(2,1)S(1)}, u32[]{:S(2)}, u32[]{:S(2)}) collective-permute-start(bf16[4,128,256]{2,1,0:T(8,128)(2,1)S(1)} %add_convert_fusion), channel_id=1, source_target_pairs={{0,1},{3,2},{1,3},{2,0},{4,5},{7,6},{5,7},{6,4},{8,9},{11,10},{9,1... | collective-permute-start | bytes 786440 | tf_op jit(solution)/shard_map/ppermute | solution.py:126
  72.0 1.5 %collective-permute-done.1 = bf16[4,128,256]{2,1,0:T(8,128)(2,1)S(1)} collective-permute-done((bf16[4,128,256]{2,1,0:T(8,128)(2,1)S(1)}, bf16[4,128,256]{2,1,0:T(8,128)(2,1)S(1)}, u32[]{:S(2)}, u32[]{:S(2)}) %collective-permute-start.1) | collective-permute-done | bytes 262176 | tf_op jit(solution)/shard_map/ppermute | solution.py:121
  73.5 0.0 collective-permute-done.4
  73.5 8.9 %collective-permute-done.3 = bf16[4,128,256]{2,1,0:T(8,128)(2,1)S(1)} collective-permute-done((bf16[4,128,256]{2,1,0:T(8,128)(2,1)S(1)}, bf16[4,128,256]{2,1,0:T(8,128)(2,1)S(1)}, u32[]{:S(2)}, u32[]{:S(2)}) %collective-permute-start.3) | collective-permute-done | bytes 262176 | tf_op jit(solution)/shard_map/ppermute | solution.py:126
  82.3 0.2 fusion
  82.5 0.9 %copy.4 = bf16[128,4,256]{2,1,0:T(4,128)(2,1)} copy(bf16[128,4,256]{2,0,1:T(8,128)(2,1)S(1)} %fusion) | data formatting | bytes 524288 | tf_op jit(solution)/shard_map/transpose | solution.py:129
Async XLA Ops:
  47.5 7.4 %collective-permute-start = (bf16[256,2048]{1,0:T(8,128)(2,1)S(1)}, bf16[256,2048]{1,0:T(8,128)(2,1)S(1)}, u32[]{:S(2)}, u32[]{:S(2)}) collective-permute-start(bf16[256,2048]{1,0:T(8,128)(2,1)S(1)} %bitcast.8), channel_id=1, source_target_pairs={{0,4},{4,0},{1,5},{5,1},{2,6},{6,2},{3,7},{7,3},{8,12},{12,8},{9,1... | collective-permute-start | bytes 3145736 | tf_op jit(solution)/shard_map/ppermute | solution.py:109
  52.7 2.3 %copy-start = (bf16[4,2048]{1,0:T(4,128)(2,1)S(1)}, bf16[4,2048]{1,0:T(4,128)(2,1)}, u32[]{:S(2)}) copy-start(bf16[4,2048]{1,0:T(4,128)(2,1)} %get-tuple-element.11.refs_1_) | copy-start | bytes 49156
  57.4 12.1 %collective-permute-start.2 = (bf16[4,128,256]{2,1,0:T(8,128)(2,1)S(1)}, bf16[4,128,256]{2,1,0:T(8,128)(2,1)S(1)}, u32[]{:S(2)}, u32[]{:S(2)}) collective-permute-start(bf16[4,128,256]{2,1,0:T(8,128)(2,1)S(1)} %get-tuple-element.16), channel_id=1, source_target_pairs={{0,1},{3,2},{4,5},{7,6},{8,9},{11,10},{12,13},{15,14},{16,17},{19,... | collective-permute-start | bytes 786440 | tf_op jit(solution)/shard_map/ppermute | solution.py:122
  62.6 10.8 %collective-permute-start.4 = (bf16[4,128,256]{2,1,0:T(8,128)(2,1)S(1)}, bf16[4,128,256]{2,1,0:T(8,128)(2,1)S(1)}, u32[]{:S(2)}, u32[]{:S(2)}) collective-permute-start(bf16[4,128,256]{2,1,0:T(8,128)(2,1)S(1)} %get-tuple-element.16), channel_id=1, source_target_pairs={{1,2},{2,1},{5,6},{6,5},{9,10},{10,9},{13,14},{14,13},{17,18},{18,... | collective-permute-start | bytes 786440 | tf_op jit(solution)/shard_map/ppermute | solution.py:124
  63.3 10.2 %collective-permute-start.1 = (bf16[4,128,256]{2,1,0:T(8,128)(2,1)S(1)}, bf16[4,128,256]{2,1,0:T(8,128)(2,1)S(1)}, u32[]{:S(2)}, u32[]{:S(2)}) collective-permute-start(bf16[4,128,256]{2,1,0:T(8,128)(2,1)S(1)} %get-tuple-element.14), channel_id=1, source_target_pairs={{0,2},{3,1},{1,0},{2,3},{4,6},{7,5},{5,4},{6,7},{8,10},{11,9},{9,8... | collective-permute-start | bytes 786440 | tf_op jit(solution)/shard_map/ppermute | solution.py:121
  69.5 12.8 %collective-permute-start.3 = (bf16[4,128,256]{2,1,0:T(8,128)(2,1)S(1)}, bf16[4,128,256]{2,1,0:T(8,128)(2,1)S(1)}, u32[]{:S(2)}, u32[]{:S(2)}) collective-permute-start(bf16[4,128,256]{2,1,0:T(8,128)(2,1)S(1)} %add_convert_fusion), channel_id=1, source_target_pairs={{0,1},{3,2},{1,3},{2,0},{4,5},{7,6},{5,7},{6,4},{8,9},{11,10},{9,1... | collective-permute-start | bytes 786440 | tf_op jit(solution)/shard_map/ppermute | solution.py:126

commit v6 on v5

--- a/solution.py
+++ b/solution.py
@@ -113,9 +113,11 @@
         for i in reversed(range(segments - 1)):
             value = jnp.where(seg == i, column[i], value)
         sends.append(value)
-    early = jnp.stack([tile_block[0], core] + sends[:2]).astype(jnp.int32)
+    early = jnp.stack([tile_block[0], core] + sends[:1]).astype(jnp.int32)
+    middling = jnp.stack([tile_block[0], core] + sends[1:2]).astype(jnp.int32)
     late = jnp.stack([tile_block[0], core] + sends[2:]).astype(jnp.int32)
-    near, turned = correlate(early, segments, normal, share, other)
+    (near,) = correlate(early, segments, normal, share, other)
+    (turned,) = correlate(middling, segments, normal, share, other)
     later, own = correlate(late, segments, normal, share, other)
     inner = (seg == 1) | (seg == 2)
     turned = lax.ppermute(turned, "tm", [(0, 2), (3, 1), (1, 0), (2, 3)])

time: 83.9 us -> 83.3 us (level)
  waiting for transfers between devices: 11.8 us -> 10.4 us
  Pallas kernels: 6.47 us -> 7.82 us
    pallas_call x2 -> x3, Pallas kernels: 4.85 us -> 6.19 us  [correlate(): pl.pallas_call(lambda *refs: correlate_kernel(rows, *refs), out_shape=[sh...]
    ppermute x1, waiting for transfers between devices: 8.88 us -> 8.04 us  [local(): last = lax.ppermute(later, 'tm', [(0, 1), (3, 2), (1, 3), (2, 0)])]
  transfers between devices with their start and end apart: 5 -> 5, of which waited for: 3 -> 3; matrix products, arithmetic and copies ran while one was open for 0% -> 0% of each run, Pallas kernels for 3% -> 5%
where the time goes in v6:
time: 83.3 us; the launch traced here: 82.8 us
  blocking collectives  45.7 us (55%)
  starting transfers between devices  16.6 us (20%)
  waiting for transfers between devices  10.4 us (12%)
  Pallas kernels  7.82 us (9%)
  local copies, waits for them, and re-layouts  1.09 us (1%)
    all_to_all x1, blocking collectives, local(): lax.all_to_all(sent, ('z', 'yh'), 0, 0, tiled=True)  29.1 us
    all_to_all x1, blocking collectives, local(): lax.all_to_all(sent, 'x', 0, 0, tiled=True).reshape(-1, slab.shape[1])  16.6 us
    ppermute x1, waiting for transfers between devices, local(): last = lax.ppermute(later, 'tm', [(0, 1), (3, 2), (1, 3), (2, 0)])  8.04 us
    pallas_call x3, Pallas kernels, correlate(): pl.pallas_call(lambda *refs: correlate_kernel(rows, *refs), out_shape=[sh...  6.19 us
    ppermute x1, starting transfers between devices, local(): other = lax.ppermute(share, 'core', [(0, 1), (1, 0)])  5.17 us
    ppermute x1, starting transfers between devices, local(): passed = lax.ppermute(near, 'tm', [(0, 1), (3, 2)])  5.13 us
    ppermute x1, starting transfers between devices, local(): turned = lax.ppermute(turned, 'tm', [(0, 2), (3, 1), (1, 0), (2, 3)])  3.69 us
    ppermute x1, starting transfers between devices, local(): last = lax.ppermute(later, 'tm', [(0, 1), (3, 2), (1, 3), (2, 0)])  1.92 us
  transfers between devices with their start and end apart: 5, of which 3 were waited for; matrix products, arithmetic and copies ran while one was open for 0% of the time, Pallas kernels for 5%

profile of v6, /device:TPU:1, one launch (start us, length us, event | category | flops | bytes accessed | tf_op | source)
XLA Modules:
  0.0 82.8 jit_solution(1631464100549849166)
XLA Ops:
  0.0 1.6 %normalize.1 = (bf16[4,2048]{1,0:T(4,128)(2,1)}, bf16[16,4,2048]{2,1,0:T(4,128)(2,1)}) custom-call(bf16[1,4,2048]{2,1,0:T(4,128)(2,1)} %records_ref.1, s32[4]{0:T(128)} %alive_ref.1), custom_call_target="tpu_custom_call" | custom-call | tf_op jit(solution)/shard_map/normalize/pallas_call | solution.py:33
  1.6 29.1 %all_to_all.10 = bf16[16,4,2048]{2,1,0:T(4,128)(2,1)S(1)} all-to-all(bf16[16,4,2048]{2,1,0:T(4,128)(2,1)} %get-tuple-element.10), channel_id=1, replica_groups=mesh['x'=4,'z'=8,'yh'=2,'core'=2,'tm'=4] {'z','yh'}, dimensions={0} | all-to-all | bytes 524288 | tf_op jit(solution)/shard_map/all_to_all | solution.py:106
  30.7 0.1 broadcast_in_dim.12
  30.8 0.1 broadcast_in_dim.13
  30.9 16.6 %all_to_all.11 = bf16[4,64,2048]{2,1,0:T(8,128)(2,1)S(1)} all-to-all(bf16[4,64,2048]{2,1,0:T(8,128)(2,1)S(1)} %broadcast_in_dim.13), channel_id=1, replica_groups=mesh['x'=4,'z'=8,'yh'=2,'core'=2,'tm'=4] {'x'}, dimensions={0} | all-to-all | bytes 2097152 | tf_op jit(solution)/shard_map/all_to_all | solution.py:108
  47.5 5.2 %collective-permute-start = (bf16[256,2048]{1,0:T(8,128)(2,1)S(1)}, bf16[256,2048]{1,0:T(8,128)(2,1)S(1)}, u32[]{:S(2)}, u32[]{:S(2)}) collective-permute-start(bf16[256,2048]{1,0:T(8,128)(2,1)S(1)} %bitcast.8), channel_id=1, source_target_pairs={{0,4},{4,0},{1,5},{5,1},{2,6},{6,2},{3,7},{7,3},{8,12},{12,8},{9,1... | collective-permute-start | bytes 3145736 | tf_op jit(solution)/shard_map/ppermute | solution.py:109
  52.7 0.0 copy-start
  53.4 0.1 pad_add_fusion.3.refs_0_
  53.5 0.1 pad_add_fusion.1.refs_0_
  53.5 1.4 %collective-permute-done.refs_3_ = bf16[256,2048]{1,0:T(8,128)(2,1)S(1)} collective-permute-done((bf16[256,2048]{1,0:T(8,128)(2,1)S(1)}, bf16[256,2048]{1,0:T(8,128)(2,1)S(1)}, u32[]{:S(2)}, u32[]{:S(2)}) %collective-permute-start) | collective-permute-done | bytes 1048608 | tf_op jit(solution)/shard_map/ppermute | solution.py:109
  54.9 0.0 copy-done
  54.9 1.9 %correlate.5 = bf16[4,128,256]{2,1,0:T(8,128)(2,1)S(1)} custom-call(s32[3]{0:T(128)S(1)} %pad_add_fusion.3.refs_0_, bf16[4,2048]{1,0:T(4,128)(2,1)S(1)} %copy-done, bf16[256,2048]{1,0:T(8,128)(2,1)S(1)} %bitcast.9, bf16[256,2048]{1,0:T(8,128)(2,1)S(1)} %collective-permute-done.refs_3_), custom_call_target="tpu_custom_call" | custom-call | flops 536870912 | bytes 4194304 | tf_op jit(solution)/shard_map/correlate/pallas_call | solution.py:88
  56.8 5.1 %collective-permute-start.2 = (bf16[4,128,256]{2,1,0:T(8,128)(2,1)S(1)}, bf16[4,128,256]{2,1,0:T(8,128)(2,1)S(1)}, u32[]{:S(2)}, u32[]{:S(2)}) collective-permute-start(bf16[4,128,256]{2,1,0:T(8,128)(2,1)S(1)} %correlate.5), channel_id=1, source_target_pairs={{0,1},{3,2},{4,5},{7,6},{8,9},{11,10},{12,13},{15,14},{16,17},{19,... | collective-permute-start | bytes 786440 | tf_op jit(solution)/shard_map/ppermute | solution.py:124
  62.0 0.1 pad_add_fusion.refs_0_
  62.0 0.7 collective-permute-start.4
  62.7 1.9 %correlate.4 = bf16[4,128,256]{2,1,0:T(8,128)(2,1)S(1)} custom-call(s32[3]{0:T(128)S(1)} %pad_add_fusion.1.refs_0_, bf16[4,2048]{1,0:T(4,128)(2,1)S(1)} %copy-done, bf16[256,2048]{1,0:T(8,128)(2,1)S(1)} %bitcast.10, bf16[256,2048]{1,0:T(8,128)(2,1)S(1)} %collective-permute-done.refs_3_), custom_call_target="tpu_custom_call" | custom-call | flops 536870912 | bytes 4194304 | tf_op jit(solution)/shard_map/correlate/pallas_call | solution.py:88
  64.6 3.7 %collective-permute-start.1 = (bf16[4,128,256]{2,1,0:T(8,128)(2,1)S(1)}, bf16[4,128,256]{2,1,0:T(8,128)(2,1)S(1)}, u32[]{:S(2)}, u32[]{:S(2)}) collective-permute-start(bf16[4,128,256]{2,1,0:T(8,128)(2,1)S(1)} %correlate.4), channel_id=1, source_target_pairs={{0,2},{3,1},{1,0},{2,3},{4,6},{7,5},{5,4},{6,7},{8,10},{11,9},{9,8... | collective-permute-start | bytes 786440 | tf_op jit(solution)/shard_map/ppermute | solution.py:123
  68.3 2.4 %correlate.3 = (bf16[4,128,256]{2,1,0:T(8,128)(2,1)S(1)}, bf16[4,128,256]{2,1,0:T(8,128)(2,1)S(1)}) custom-call(s32[4]{0:T(128)S(1)} %pad_add_fusion.refs_0_, bf16[4,2048]{1,0:T(4,128)(2,1)S(1)} %copy-done, bf16[256,2048]{1,0:T(8,128)(2,1)S(1)} %bitcast.11, bf16[256,2048]{1,0:T(8,128)(2,1)S(1)} %collective-permute-done.refs_3_), custom_call_target="tpu_custom_call" | custom-call | flops 1073741824 | bytes 4194304 | tf_op jit(solution)/shard_map/correlate/pallas_call | solution.py:88
  70.7 0.0 collective-permute-done.2
  70.8 0.1 add_convert_fusion
  70.8 1.9 %collective-permute-start.3 = (bf16[4,128,256]{2,1,0:T(8,128)(2,1)S(1)}, bf16[4,128,256]{2,1,0:T(8,128)(2,1)S(1)}, u32[]{:S(2)}, u32[]{:S(2)}) collective-permute-start(bf16[4,128,256]{2,1,0:T(8,128)(2,1)S(1)} %add_convert_fusion), channel_id=1, source_target_pairs={{0,1},{3,2},{1,3},{2,0},{4,5},{7,6},{5,7},{6,4},{8,9},{11,10},{9,1... | collective-permute-start | bytes 786440 | tf_op jit(solution)/shard_map/ppermute | solution.py:128
  72.8 0.9 %collective-permute-done.1 = bf16[4,128,256]{2,1,0:T(8,128)(2,1)S(1)} collective-permute-done((bf16[4,128,256]{2,1,0:T(8,128)(2,1)S(1)}, bf16[4,128,256]{2,1,0:T(8,128)(2,1)S(1)}, u32[]{:S(2)}, u32[]{:S(2)}) %collective-permute-start.1) | collective-permute-done | bytes 262176 | tf_op jit(solution)/shard_map/ppermute | solution.py:123
  73.7 0.0 collective-permute-done.4
  73.7 8.0 %collective-permute-done.3 = bf16[4,128,256]{2,1,0:T(8,128)(2,1)S(1)} collective-permute-done((bf16[4,128,256]{2,1,0:T(8,128)(2,1)S(1)}, bf16[4,128,256]{2,1,0:T(8,128)(2,1)S(1)}, u32[]{:S(2)}, u32[]{:S(2)}) %collective-permute-start.3) | collective-permute-done | bytes 262176 | tf_op jit(solution)/shard_map/ppermute | solution.py:128
  81.7 0.2 fusion
  81.9 0.9 %copy.4 = bf16[128,4,256]{2,1,0:T(4,128)(2,1)} copy(bf16[128,4,256]{2,0,1:T(8,128)(2,1)S(1)} %fusion) | data formatting | bytes 524288 | tf_op jit(solution)/shard_map/transpose | solution.py:131
Async XLA Ops:
  47.5 7.4 %collective-permute-start = (bf16[256,2048]{1,0:T(8,128)(2,1)S(1)}, bf16[256,2048]{1,0:T(8,128)(2,1)S(1)}, u32[]{:S(2)}, u32[]{:S(2)}) collective-permute-start(bf16[256,2048]{1,0:T(8,128)(2,1)S(1)} %bitcast.8), channel_id=1, source_target_pairs={{0,4},{4,0},{1,5},{5,1},{2,6},{6,2},{3,7},{7,3},{8,12},{12,8},{9,1... | collective-permute-start | bytes 3145736 | tf_op jit(solution)/shard_map/ppermute | solution.py:109
  52.7 2.2 %copy-start = (bf16[4,2048]{1,0:T(4,128)(2,1)S(1)}, bf16[4,2048]{1,0:T(4,128)(2,1)}, u32[]{:S(2)}) copy-start(bf16[4,2048]{1,0:T(4,128)(2,1)} %get-tuple-element.9.refs_1_) | copy-start | bytes 49156
  56.8 13.9 %collective-permute-start.2 = (bf16[4,128,256]{2,1,0:T(8,128)(2,1)S(1)}, bf16[4,128,256]{2,1,0:T(8,128)(2,1)S(1)}, u32[]{:S(2)}, u32[]{:S(2)}) collective-permute-start(bf16[4,128,256]{2,1,0:T(8,128)(2,1)S(1)} %correlate.5), channel_id=1, source_target_pairs={{0,1},{3,2},{4,5},{7,6},{8,9},{11,10},{12,13},{15,14},{16,17},{19,... | collective-permute-start | bytes 786440 | tf_op jit(solution)/shard_map/ppermute | solution.py:124
  62.0 11.7 %collective-permute-start.4 = (bf16[4,128,256]{2,1,0:T(8,128)(2,1)S(1)}, bf16[4,128,256]{2,1,0:T(8,128)(2,1)S(1)}, u32[]{:S(2)}, u32[]{:S(2)}) collective-permute-start(bf16[4,128,256]{2,1,0:T(8,128)(2,1)S(1)} %correlate.5), channel_id=1, source_target_pairs={{1,2},{2,1},{5,6},{6,5},{9,10},{10,9},{13,14},{14,13},{17,18},{18,... | collective-permute-start | bytes 786440 | tf_op jit(solution)/shard_map/ppermute | solution.py:126
  64.6 9.1 %collective-permute-start.1 = (bf16[4,128,256]{2,1,0:T(8,128)(2,1)S(1)}, bf16[4,128,256]{2,1,0:T(8,128)(2,1)S(1)}, u32[]{:S(2)}, u32[]{:S(2)}) collective-permute-start(bf16[4,128,256]{2,1,0:T(8,128)(2,1)S(1)} %correlate.4), channel_id=1, source_target_pairs={{0,2},{3,1},{1,0},{2,3},{4,6},{7,5},{5,4},{6,7},{8,10},{11,9},{9,8... | collective-permute-start | bytes 786440 | tf_op jit(solution)/shard_map/ppermute | solution.py:123
  70.8 10.9 %collective-permute-start.3 = (bf16[4,128,256]{2,1,0:T(8,128)(2,1)S(1)}, bf16[4,128,256]{2,1,0:T(8,128)(2,1)S(1)}, u32[]{:S(2)}, u32[]{:S(2)}) collective-permute-start(bf16[4,128,256]{2,1,0:T(8,128)(2,1)S(1)} %add_convert_fusion), channel_id=1, source_target_pairs={{0,1},{3,2},{1,3},{2,0},{4,5},{7,6},{5,7},{6,4},{8,9},{11,10},{9,1... | collective-permute-start | bytes 786440 | tf_op jit(solution)/shard_map/ppermute | solution.py:128

commit v7 on v5

--- a/solution.py
+++ b/solution.py
@@ -113,10 +113,14 @@
         for i in reversed(range(segments - 1)):
             value = jnp.where(seg == i, column[i], value)
         sends.append(value)
-    early = jnp.stack([tile_block[0], core] + sends[:2]).astype(jnp.int32)
-    late = jnp.stack([tile_block[0], core] + sends[2:]).astype(jnp.int32)
-    near, turned = correlate(early, segments, normal, share, other)
-    later, own = correlate(late, segments, normal, share, other)
+    def chunks(*owners):
+        where = jnp.stack([tile_block[0], core] + list(owners)).astype(jnp.int32)
+        return correlate(where, segments, normal, share, other)
+
+    (near,) = chunks(*sends[0:1])
+    (turned,) = chunks(*sends[1:2])
+    (later,) = chunks(*sends[2:3])
+    (own,) = chunks(*sends[3:4])
     inner = (seg == 1) | (seg == 2)
     turned = lax.ppermute(turned, "tm", [(0, 2), (3, 1), (1, 0), (2, 3)])
     passed = lax.ppermute(near, "tm", [(0, 1), (3, 2)])

time: 83.9 us -> 83.5 us (level)
  Pallas kernels: 6.47 us -> 9.17 us
  waiting for transfers between devices: 11.8 us -> 9.31 us
    pallas_call x2 -> x4, Pallas kernels: 4.85 us -> 7.55 us  [correlate(): pl.pallas_call(lambda *refs: correlate_kernel(rows, *refs), out_shape=[sh...]
    ppermute x1, waiting for transfers between devices: 1.46 us -> 0.01 us  [local(): turned = lax.ppermute(turned, 'tm', [(0, 2), (3, 1), (1, 0), (2, 3)])]
    ppermute x1, waiting for transfers between devices: 8.88 us -> 7.89 us  [local(): last = lax.ppermute(later, 'tm', [(0, 1), (3, 2), (1, 3), (2, 0)])]
  transfers between devices with their start and end apart: 5 -> 5, of which waited for: 3 -> 2; matrix products, arithmetic and copies ran while one was open for 0% -> 0% of each run, Pallas kernels for 3% -> 7%
where the time goes in v7:
time: 83.5 us; the launch traced here: 83.1 us
  blocking collectives  45.7 us (55%)
  starting transfers between devices  16.6 us (20%)
  waiting for transfers between devices  9.31 us (11%)
  Pallas kernels  9.17 us (11%)
  local copies, waits for them, and re-layouts  1.09 us (1%)
    all_to_all x1, blocking collectives, local(): lax.all_to_all(sent, ('z', 'yh'), 0, 0, tiled=True)  29.1 us
    all_to_all x1, blocking collectives, local(): lax.all_to_all(sent, 'x', 0, 0, tiled=True).reshape(-1, slab.shape[1])  16.6 us
    ppermute x1, waiting for transfers between devices, local(): last = lax.ppermute(later, 'tm', [(0, 1), (3, 2), (1, 3), (2, 0)])  7.89 us
    pallas_call x4, Pallas kernels, correlate(): pl.pallas_call(lambda *refs: correlate_kernel(rows, *refs), out_shape=[sh...  7.55 us
    ppermute x1, starting transfers between devices, local(): other = lax.ppermute(share, 'core', [(0, 1), (1, 0)])  5.17 us
    ppermute x1, starting transfers between devices, local(): passed = lax.ppermute(near, 'tm', [(0, 1), (3, 2)])  5.13 us
    ppermute x1, starting transfers between devices, local(): turned = lax.ppermute(turned, 'tm', [(0, 2), (3, 1), (1, 0), (2, 3)])  3.68 us
    ppermute x1, starting transfers between devices, local(): last = lax.ppermute(later, 'tm', [(0, 1), (3, 2), (1, 3), (2, 0)])  1.92 us
  transfers between devices with their start and end apart: 5, of which 2 were waited for; matrix products, arithmetic and copies ran while one was open for 0% of the time, Pallas kernels for 7%

profile of v7, /device:TPU:1, one launch (start us, length us, event | category | flops | bytes accessed | tf_op | source)
XLA Modules:
  0.0 83.1 jit_solution(6067254883325992589)
XLA Ops:
  0.0 1.6 %normalize.1 = (bf16[4,2048]{1,0:T(4,128)(2,1)}, bf16[16,4,2048]{2,1,0:T(4,128)(2,1)}) custom-call(bf16[1,4,2048]{2,1,0:T(4,128)(2,1)} %records_ref.1, s32[4]{0:T(128)} %alive_ref.1), custom_call_target="tpu_custom_call" | custom-call | tf_op jit(solution)/shard_map/normalize/pallas_call | solution.py:33
  1.6 29.1 %all_to_all.10 = bf16[16,4,2048]{2,1,0:T(4,128)(2,1)S(1)} all-to-all(bf16[16,4,2048]{2,1,0:T(4,128)(2,1)} %get-tuple-element.8), channel_id=1, replica_groups=mesh['x'=4,'z'=8,'yh'=2,'core'=2,'tm'=4] {'z','yh'}, dimensions={0} | all-to-all | bytes 524288 | tf_op jit(solution)/shard_map/all_to_all | solution.py:106
  30.7 0.1 broadcast_in_dim.12
  30.8 0.1 broadcast_in_dim.13
  30.9 16.6 %all_to_all.11 = bf16[4,64,2048]{2,1,0:T(8,128)(2,1)S(1)} all-to-all(bf16[4,64,2048]{2,1,0:T(8,128)(2,1)S(1)} %broadcast_in_dim.13), channel_id=1, replica_groups=mesh['x'=4,'z'=8,'yh'=2,'core'=2,'tm'=4] {'x'}, dimensions={0} | all-to-all | bytes 2097152 | tf_op jit(solution)/shard_map/all_to_all | solution.py:108
  47.5 5.2 %collective-permute-start = (bf16[256,2048]{1,0:T(8,128)(2,1)S(1)}, bf16[256,2048]{1,0:T(8,128)(2,1)S(1)}, u32[]{:S(2)}, u32[]{:S(2)}) collective-permute-start(bf16[256,2048]{1,0:T(8,128)(2,1)S(1)} %bitcast.8), channel_id=1, source_target_pairs={{0,4},{4,0},{1,5},{5,1},{2,6},{6,2},{3,7},{7,3},{8,12},{12,8},{9,1... | collective-permute-start | bytes 3145736 | tf_op jit(solution)/shard_map/ppermute | solution.py:109
  52.7 0.0 copy-start
  53.4 0.1 pad_add_fusion
  53.5 0.1 pad_add_fusion.2
  53.5 1.4 %collective-permute-done.refs_3_ = bf16[256,2048]{1,0:T(8,128)(2,1)S(1)} collective-permute-done((bf16[256,2048]{1,0:T(8,128)(2,1)S(1)}, bf16[256,2048]{1,0:T(8,128)(2,1)S(1)}, u32[]{:S(2)}, u32[]{:S(2)}) %collective-permute-start) | collective-permute-done | bytes 1048608 | tf_op jit(solution)/shard_map/ppermute | solution.py:109
  54.9 0.0 copy-done
  54.9 1.9 %correlate.7 = bf16[4,128,256]{2,1,0:T(8,128)(2,1)S(1)} custom-call(s32[3]{0:T(128)S(1)} %get-tuple-element.13.refs_0_, bf16[4,2048]{1,0:T(4,128)(2,1)S(1)} %copy-done, bf16[256,2048]{1,0:T(8,128)(2,1)S(1)} %bitcast.9, bf16[256,2048]{1,0:T(8,128)(2,1)S(1)} %collective-permute-done.refs_3_), custom_call_target="tpu_custom_call" | custom-call | flops 536870912 | bytes 4194304 | tf_op jit(solution)/shard_map/correlate/pallas_call | solution.py:88
  56.8 5.1 %collective-permute-start.2 = (bf16[4,128,256]{2,1,0:T(8,128)(2,1)S(1)}, bf16[4,128,256]{2,1,0:T(8,128)(2,1)S(1)}, u32[]{:S(2)}, u32[]{:S(2)}) collective-permute-start(bf16[4,128,256]{2,1,0:T(8,128)(2,1)S(1)} %correlate.7), channel_id=1, source_target_pairs={{0,1},{3,2},{4,5},{7,6},{8,9},{11,10},{12,13},{15,14},{16,17},{19,... | collective-permute-start | bytes 786440 | tf_op jit(solution)/shard_map/ppermute | solution.py:126
  62.0 0.7 collective-permute-start.4
  62.6 1.9 %correlate.5 = bf16[4,128,256]{2,1,0:T(8,128)(2,1)S(1)} custom-call(s32[3]{0:T(128)S(1)} %get-tuple-element.11.refs_0_, bf16[4,2048]{1,0:T(4,128)(2,1)S(1)} %copy-done, bf16[256,2048]{1,0:T(8,128)(2,1)S(1)} %bitcast.10, bf16[256,2048]{1,0:T(8,128)(2,1)S(1)} %collective-permute-done.refs_3_), custom_call_target="tpu_custom_call" | custom-call | flops 536870912 | bytes 4194304 | tf_op jit(solution)/shard_map/correlate/pallas_call | solution.py:88
  64.5 3.7 %collective-permute-start.1 = (bf16[4,128,256]{2,1,0:T(8,128)(2,1)S(1)}, bf16[4,128,256]{2,1,0:T(8,128)(2,1)S(1)}, u32[]{:S(2)}, u32[]{:S(2)}) collective-permute-start(bf16[4,128,256]{2,1,0:T(8,128)(2,1)S(1)} %correlate.5), channel_id=1, source_target_pairs={{0,2},{3,1},{1,0},{2,3},{4,6},{7,5},{5,4},{6,7},{8,10},{11,9},{9,8... | collective-permute-start | bytes 786440 | tf_op jit(solution)/shard_map/ppermute | solution.py:125
  68.2 1.9 %correlate.6 = bf16[4,128,256]{2,1,0:T(8,128)(2,1)S(1)} custom-call(s32[3]{0:T(128)S(1)} %get-tuple-element.12.refs_0_, bf16[4,2048]{1,0:T(4,128)(2,1)S(1)} %copy-done, bf16[256,2048]{1,0:T(8,128)(2,1)S(1)} %bitcast.11, bf16[256,2048]{1,0:T(8,128)(2,1)S(1)} %collective-permute-done.refs_3_), custom_call_target="tpu_custom_call" | custom-call | flops 536870912 | bytes 4194304 | tf_op jit(solution)/shard_map/correlate/pallas_call | solution.py:88
  70.1 0.0 collective-permute-done.2
  70.2 0.1 add_convert_fusion
  70.2 1.9 %collective-permute-start.3 = (bf16[4,128,256]{2,1,0:T(8,128)(2,1)S(1)}, bf16[4,128,256]{2,1,0:T(8,128)(2,1)S(1)}, u32[]{:S(2)}, u32[]{:S(2)}) collective-permute-start(bf16[4,128,256]{2,1,0:T(8,128)(2,1)S(1)} %add_convert_fusion), channel_id=1, source_target_pairs={{0,1},{3,2},{1,3},{2,0},{4,5},{7,6},{5,7},{6,4},{8,9},{11,10},{9,1... | collective-permute-start | bytes 786440 | tf_op jit(solution)/shard_map/ppermute | solution.py:130
  72.2 1.9 %correlate.4 = bf16[4,128,256]{2,1,0:T(8,128)(2,1)S(1)} custom-call(s32[3]{0:T(128)S(1)} %get-tuple-element.9.refs_0_, bf16[4,2048]{1,0:T(4,128)(2,1)S(1)} %copy-done, bf16[256,2048]{1,0:T(8,128)(2,1)S(1)} %bitcast.12, bf16[256,2048]{1,0:T(8,128)(2,1)S(1)} %collective-permute-done.refs_3_), custom_call_target="tpu_custom_call" | custom-call | flops 536870912 | bytes 4194304 | tf_op jit(solution)/shard_map/correlate/pallas_call | solution.py:88
  74.1 0.0 collective-permute-done.1
  74.1 0.0 collective-permute-done.4
  74.1 7.9 %collective-permute-done.3 = bf16[4,128,256]{2,1,0:T(8,128)(2,1)S(1)} collective-permute-done((bf16[4,128,256]{2,1,0:T(8,128)(2,1)S(1)}, bf16[4,128,256]{2,1,0:T(8,128)(2,1)S(1)}, u32[]{:S(2)}, u32[]{:S(2)}) %collective-permute-start.3) | collective-permute-done | bytes 262176 | tf_op jit(solution)/shard_map/ppermute | solution.py:130
  82.0 0.2 fusion
  82.2 0.9 %copy.4 = bf16[128,4,256]{2,1,0:T(4,128)(2,1)} copy(bf16[128,4,256]{2,0,1:T(8,128)(2,1)S(1)} %fusion) | data formatting | bytes 524288 | tf_op jit(solution)/shard_map/transpose | solution.py:133
Async XLA Ops:
  47.5 7.4 %collective-permute-start = (bf16[256,2048]{1,0:T(8,128)(2,1)S(1)}, bf16[256,2048]{1,0:T(8,128)(2,1)S(1)}, u32[]{:S(2)}, u32[]{:S(2)}) collective-permute-start(bf16[256,2048]{1,0:T(8,128)(2,1)S(1)} %bitcast.8), channel_id=1, source_target_pairs={{0,4},{4,0},{1,5},{5,1},{2,6},{6,2},{3,7},{7,3},{8,12},{12,8},{9,1... | collective-permute-start | bytes 3145736 | tf_op jit(solution)/shard_map/ppermute | solution.py:109
  52.7 2.2 %copy-start = (bf16[4,2048]{1,0:T(4,128)(2,1)S(1)}, bf16[4,2048]{1,0:T(4,128)(2,1)}, u32[]{:S(2)}) copy-start(bf16[4,2048]{1,0:T(4,128)(2,1)} %get-tuple-element.7.refs_1_) | copy-start | bytes 49156
  56.8 13.3 %collective-permute-start.2 = (bf16[4,128,256]{2,1,0:T(8,128)(2,1)S(1)}, bf16[4,128,256]{2,1,0:T(8,128)(2,1)S(1)}, u32[]{:S(2)}, u32[]{:S(2)}) collective-permute-start(bf16[4,128,256]{2,1,0:T(8,128)(2,1)S(1)} %correlate.7), channel_id=1, source_target_pairs={{0,1},{3,2},{4,5},{7,6},{8,9},{11,10},{12,13},{15,14},{16,17},{19,... | collective-permute-start | bytes 786440 | tf_op jit(solution)/shard_map/ppermute | solution.py:126
  62.0 12.1 %collective-permute-start.4 = (bf16[4,128,256]{2,1,0:T(8,128)(2,1)S(1)}, bf16[4,128,256]{2,1,0:T(8,128)(2,1)S(1)}, u32[]{:S(2)}, u32[]{:S(2)}) collective-permute-start(bf16[4,128,256]{2,1,0:T(8,128)(2,1)S(1)} %correlate.7), channel_id=1, source_target_pairs={{1,2},{2,1},{5,6},{6,5},{9,10},{10,9},{13,14},{14,13},{17,18},{18,... | collective-permute-start | bytes 786440 | tf_op jit(solution)/shard_map/ppermute | solution.py:128
  64.5 9.5 %collective-permute-start.1 = (bf16[4,128,256]{2,1,0:T(8,128)(2,1)S(1)}, bf16[4,128,256]{2,1,0:T(8,128)(2,1)S(1)}, u32[]{:S(2)}, u32[]{:S(2)}) collective-permute-start(bf16[4,128,256]{2,1,0:T(8,128)(2,1)S(1)} %correlate.5), channel_id=1, source_target_pairs={{0,2},{3,1},{1,0},{2,3},{4,6},{7,5},{5,4},{6,7},{8,10},{11,9},{9,8... | collective-permute-start | bytes 786440 | tf_op jit(solution)/shard_map/ppermute | solution.py:125
  70.2 11.7 %collective-permute-start.3 = (bf16[4,128,256]{2,1,0:T(8,128)(2,1)S(1)}, bf16[4,128,256]{2,1,0:T(8,128)(2,1)S(1)}, u32[]{:S(2)}, u32[]{:S(2)}) collective-permute-start(bf16[4,128,256]{2,1,0:T(8,128)(2,1)S(1)} %add_convert_fusion), channel_id=1, source_target_pairs={{0,1},{3,2},{1,3},{2,0},{4,5},{7,6},{5,7},{6,4},{8,9},{11,10},{9,1... | collective-permute-start | bytes 786440 | tf_op jit(solution)/shard_map/ppermute | solution.py:130

commit v8 on v5

--- a/solution.py
+++ b/solution.py
@@ -43,21 +43,21 @@
 
 
 def correlate_kernel(rows, where_ref, own_ref, mine_ref, other_ref, *rest):
-    out_refs, skew_ref, cols_ref = rest[:-2], rest[-2], rest[-1]
-    samples, width = own_ref.shape[1], skew_ref.shape[1]
+    out_ref, line_ref, skew_ref, cols_ref = rest
+    samples = own_ref.shape[1]
     chunk = skew_ref.shape[0] // rows
     cols = cols_ref.shape[0]
     half = cols // 2
-    last = (width - samples) // chunk
+    last = LAGS // chunk - 1
     block, core = where_ref[0], where_ref[1]
+    start = pl.multiple_of(chunk * (last - where_ref[2]), chunk)
+    line_ref[...] = jnp.zeros(line_ref.shape, jnp.float32)
+    line_ref[:, pl.ds(2 * chunk, samples)] = own_ref[...].astype(jnp.float32)
     for c in range(rows):
-        line = own_ref[pl.ds(c, 1), :].astype(jnp.float32)
-        line = jnp.concatenate(
-            [jnp.zeros((1, chunk), jnp.float32), line, jnp.zeros((1, width - samples - chunk), jnp.float32)], axis=1
-        )
-        grid = jnp.broadcast_to(line, (chunk, width))
+        line = line_ref[pl.ds(c, 1), pl.ds(start, samples + chunk)]
+        grid = jnp.broadcast_to(line, (chunk, samples + chunk))
         skewed = pltpu.roll(grid, 0, 1, stride=1, stride_axis=0)
-        skew_ref[pl.ds(c * chunk, chunk), :] = skewed.astype(jnp.bfloat16)
+        skew_ref[pl.ds(c * chunk, chunk), :] = skewed[:, chunk:].astype(jnp.bfloat16)
     first = block * half
     group = 2 * rows
     upper = lax.broadcasted_iota(jnp.int32, (group, samples), 0) < rows
@@ -70,30 +70,29 @@
             e, o = even[part * group : (part + 1) * group], odd[part * group : (part + 1) * group]
             woven += [jnp.where(upper, e, pltpu.roll(o, rows, 0)), jnp.where(upper, pltpu.roll(e, rows, 0), o)]
         cols_ref[pl.ds(2 * at, 4 * group), :] = jnp.concatenate(woven, axis=0).astype(jnp.bfloat16)
-    for i, out_ref in enumerate(out_refs):
-        window = pl.ds(pl.multiple_of(chunk * (last - where_ref[2 + i]), chunk), samples)
-        total = lax.dot_general(
-            skew_ref[:, window], cols_ref[...], (((1,), (1,)), ((), ())), preferred_element_type=jnp.float32
-        )
-        out_ref[...] = total.astype(jnp.bfloat16).reshape(out_ref.shape)
+    total = lax.dot_general(
+        skew_ref[...], cols_ref[...], (((1,), (1,)), ((), ())), preferred_element_type=jnp.float32
+    )
+    out_ref[...] = total.astype(jnp.bfloat16).reshape(out_ref.shape)
 
 
 def correlate(where, segments, own, mine, other):
     rows, samples = own.shape
-    count = where.shape[0] - 2
     chunk = LAGS // segments
-    width = samples + LAGS - chunk
     cols = 2 * mine.shape[0] // NBLK
-    shape = jax.ShapeDtypeStruct((rows, chunk, cols), jnp.bfloat16)
     return pl.pallas_call(
         lambda *refs: correlate_kernel(rows, *refs),
-        out_shape=[shape] * count,
+        out_shape=jax.ShapeDtypeStruct((rows, chunk, cols), jnp.bfloat16),
         in_specs=[SMEM, VMEM, VMEM, VMEM],
-        out_specs=[VMEM] * count,
-        scratch_shapes=[pltpu.VMEM((rows * chunk, width), jnp.bfloat16), pltpu.VMEM((cols, samples), jnp.bfloat16)],
+        out_specs=VMEM,
+        scratch_shapes=[
+            pltpu.VMEM((rows, samples + LAGS), jnp.float32),
+            pltpu.VMEM((rows * chunk, samples), jnp.bfloat16),
+            pltpu.VMEM((cols, samples), jnp.bfloat16),
+        ],
         compiler_params=pltpu.CompilerParams(vmem_limit_bytes=40 * MiB),
         cost_estimate=pl.CostEstimate(
-            flops=2 * rows * count * chunk * samples * cols, bytes_accessed=4 * MiB, transcendentals=0
+            flops=2 * rows * chunk * samples * cols, bytes_accessed=4 * MiB, transcendentals=0
         ),
         name="correlate",
     )(where, own, mine, other)
@@ -113,10 +112,10 @@
         for i in reversed(range(segments - 1)):
             value = jnp.where(seg == i, column[i], value)
         sends.append(value)
-    early = jnp.stack([tile_block[0], core] + sends[:2]).astype(jnp.int32)
-    late = jnp.stack([tile_block[0], core] + sends[2:]).astype(jnp.int32)
-    near, turned = correlate(early, segments, normal, share, other)
-    later, own = correlate(late, segments, normal, share, other)
+    near, turned, later, own = (
+        correlate(jnp.stack([tile_block[0], core, owner]).astype(jnp.int32), segments, normal, share, other)
+        for owner in sends
+    )
     inner = (seg == 1) | (seg == 2)
     turned = lax.ppermute(turned, "tm", [(0, 2), (3, 1), (1, 0), (2, 3)])
     passed = lax.ppermute(near, "tm", [(0, 1), (3, 2)])

time: 83.9 us -> 83 us (0.989)
  waiting for transfers between devices: 11.8 us -> 9.81 us
  Pallas kernels: 6.47 us -> 8.16 us
    pallas_call x2 -> x4, Pallas kernels: 4.85 us -> 6.54 us  [correlate(): pl.pallas_call(lambda *refs: correlate_kernel(rows, *refs), out_shape=jax...]
    ppermute x1, waiting for transfers between devices: 1.46 us -> 0.08 us  [local(): turned = lax.ppermute(turned, 'tm', [(0, 2), (3, 1), (1, 0), (2, 3)])]
  transfers between devices with their start and end apart: 5 -> 5, of which waited for: 3 -> 3; matrix products, arithmetic and copies ran while one was open for 0% -> 0% of each run, Pallas kernels for 3% -> 6%
where the time goes in v8:
time: 83 us; the launch traced here: 82.5 us
  blocking collectives  45.7 us (55%)
  starting transfers between devices  16.6 us (20%)
  waiting for transfers between devices  9.81 us (12%)
  Pallas kernels  8.16 us (10%)
  local copies, waits for them, and re-layouts  1.09 us (1%)
    all_to_all x1, blocking collectives, local(): lax.all_to_all(sent, ('z', 'yh'), 0, 0, tiled=True)  29.1 us
    all_to_all x1, blocking collectives, local(): lax.all_to_all(sent, 'x', 0, 0, tiled=True).reshape(-1, slab.shape[1])  16.6 us
    ppermute x1, waiting for transfers between devices, local(): last = lax.ppermute(later, 'tm', [(0, 1), (3, 2), (1, 3), (2, 0)])  8.31 us
    pallas_call x4, Pallas kernels, correlate(): pl.pallas_call(lambda *refs: correlate_kernel(rows, *refs), out_shape=jax...  6.54 us
    ppermute x1, starting transfers between devices, local(): other = lax.ppermute(share, 'core', [(0, 1), (1, 0)])  5.17 us
    ppermute x1, starting transfers between devices, local(): passed = lax.ppermute(near, 'tm', [(0, 1), (3, 2)])  5.11 us
    ppermute x1, starting transfers between devices, local(): turned = lax.ppermute(turned, 'tm', [(0, 2), (3, 1), (1, 0), (2, 3)])  3.69 us
    ppermute x1, starting transfers between devices, local(): last = lax.ppermute(later, 'tm', [(0, 1), (3, 2), (1, 3), (2, 0)])  1.92 us
  transfers between devices with their start and end apart: 5, of which 3 were waited for; matrix products, arithmetic and copies ran while one was open for 0% of the time, Pallas kernels for 6%

profile of v8, /device:TPU:1, one launch (start us, length us, event | category | flops | bytes accessed | tf_op | source)
XLA Modules:
  0.0 82.5 jit_solution(7892161884585776115)
XLA Ops:
  0.0 1.6 %normalize.1 = (bf16[4,2048]{1,0:T(4,128)(2,1)}, bf16[16,4,2048]{2,1,0:T(4,128)(2,1)}) custom-call(bf16[1,4,2048]{2,1,0:T(4,128)(2,1)} %records_ref.1, s32[4]{0:T(128)} %alive_ref.1), custom_call_target="tpu_custom_call" | custom-call | tf_op jit(solution)/shard_map/normalize/pallas_call | solution.py:33
  1.6 29.1 %all_to_all.10 = bf16[16,4,2048]{2,1,0:T(4,128)(2,1)S(1)} all-to-all(bf16[16,4,2048]{2,1,0:T(4,128)(2,1)} %get-tuple-element.8), channel_id=1, replica_groups=mesh['x'=4,'z'=8,'yh'=2,'core'=2,'tm'=4] {'z','yh'}, dimensions={0} | all-to-all | bytes 524288 | tf_op jit(solution)/shard_map/all_to_all | solution.py:105
  30.7 0.1 broadcast_in_dim.12
  30.8 0.1 broadcast_in_dim.13
  30.9 16.6 %all_to_all.11 = bf16[4,64,2048]{2,1,0:T(8,128)(2,1)S(1)} all-to-all(bf16[4,64,2048]{2,1,0:T(8,128)(2,1)S(1)} %broadcast_in_dim.13), channel_id=1, replica_groups=mesh['x'=4,'z'=8,'yh'=2,'core'=2,'tm'=4] {'x'}, dimensions={0} | all-to-all | bytes 2097152 | tf_op jit(solution)/shard_map/all_to_all | solution.py:107
  47.5 5.2 %collective-permute-start = (bf16[256,2048]{1,0:T(8,128)(2,1)S(1)}, bf16[256,2048]{1,0:T(8,128)(2,1)S(1)}, u32[]{:S(2)}, u32[]{:S(2)}) collective-permute-start(bf16[256,2048]{1,0:T(8,128)(2,1)S(1)} %bitcast.8), channel_id=1, source_target_pairs={{0,4},{4,0},{1,5},{5,1},{2,6},{6,2},{3,7},{7,3},{8,12},{12,8},{9,1... | collective-permute-start | bytes 3145736 | tf_op jit(solution)/shard_map/ppermute | solution.py:108
  52.7 0.0 copy-start
  53.4 0.1 pad_add_fusion
  53.5 0.1 pad_add_fusion.2
  53.5 1.4 %collective-permute-done.refs_3_ = bf16[256,2048]{1,0:T(8,128)(2,1)S(1)} collective-permute-done((bf16[256,2048]{1,0:T(8,128)(2,1)S(1)}, bf16[256,2048]{1,0:T(8,128)(2,1)S(1)}, u32[]{:S(2)}, u32[]{:S(2)}) %collective-permute-start) | collective-permute-done | bytes 1048608 | tf_op jit(solution)/shard_map/ppermute | solution.py:108
  54.9 0.0 copy-done
  54.9 1.6 %correlate.7 = bf16[4,128,256]{2,1,0:T(8,128)(2,1)S(1)} custom-call(s32[3]{0:T(128)S(1)} %get-tuple-element.13.refs_0_, bf16[4,2048]{1,0:T(4,128)(2,1)S(1)} %copy-done, bf16[256,2048]{1,0:T(8,128)(2,1)S(1)} %bitcast.9, bf16[256,2048]{1,0:T(8,128)(2,1)S(1)} %collective-permute-done.refs_3_), custom_call_target="tpu_custom_call" | custom-call | flops 536870912 | bytes 4194304 | tf_op jit(solution)/shard_map/correlate/pallas_call | solution.py:83
  56.6 5.1 %collective-permute-start.2 = (bf16[4,128,256]{2,1,0:T(8,128)(2,1)S(1)}, bf16[4,128,256]{2,1,0:T(8,128)(2,1)S(1)}, u32[]{:S(2)}, u32[]{:S(2)}) collective-permute-start(bf16[4,128,256]{2,1,0:T(8,128)(2,1)S(1)} %correlate.7), channel_id=1, source_target_pairs={{0,1},{3,2},{4,5},{7,6},{8,9},{11,10},{12,13},{15,14},{16,17},{19,... | collective-permute-start | bytes 786440 | tf_op jit(solution)/shard_map/ppermute | solution.py:121
  61.7 0.7 collective-permute-start.4
  62.4 1.6 %correlate.5 = bf16[4,128,256]{2,1,0:T(8,128)(2,1)S(1)} custom-call(s32[3]{0:T(128)S(1)} %get-tuple-element.11.refs_0_, bf16[4,2048]{1,0:T(4,128)(2,1)S(1)} %copy-done, bf16[256,2048]{1,0:T(8,128)(2,1)S(1)} %bitcast.10, bf16[256,2048]{1,0:T(8,128)(2,1)S(1)} %collective-permute-done.refs_3_), custom_call_target="tpu_custom_call" | custom-call | flops 536870912 | bytes 4194304 | tf_op jit(solution)/shard_map/correlate/pallas_call | solution.py:83
  64.0 3.7 %collective-permute-start.1 = (bf16[4,128,256]{2,1,0:T(8,128)(2,1)S(1)}, bf16[4,128,256]{2,1,0:T(8,128)(2,1)S(1)}, u32[]{:S(2)}, u32[]{:S(2)}) collective-permute-start(bf16[4,128,256]{2,1,0:T(8,128)(2,1)S(1)} %correlate.5), channel_id=1, source_target_pairs={{0,2},{3,1},{1,0},{2,3},{4,6},{7,5},{5,4},{6,7},{8,10},{11,9},{9,8... | collective-permute-start | bytes 786440 | tf_op jit(solution)/shard_map/ppermute | solution.py:120
  67.7 1.6 %correlate.6 = bf16[4,128,256]{2,1,0:T(8,128)(2,1)S(1)} custom-call(s32[3]{0:T(128)S(1)} %get-tuple-element.12.refs_0_, bf16[4,2048]{1,0:T(4,128)(2,1)S(1)} %copy-done, bf16[256,2048]{1,0:T(8,128)(2,1)S(1)} %bitcast.11, bf16[256,2048]{1,0:T(8,128)(2,1)S(1)} %collective-permute-done.refs_3_), custom_call_target="tpu_custom_call" | custom-call | flops 536870912 | bytes 4194304 | tf_op jit(solution)/shard_map/correlate/pallas_call | solution.py:83
  69.4 0.0 collective-permute-done.2
  69.4 0.1 add_convert_fusion
  69.5 1.9 %collective-permute-start.3 = (bf16[4,128,256]{2,1,0:T(8,128)(2,1)S(1)}, bf16[4,128,256]{2,1,0:T(8,128)(2,1)S(1)}, u32[]{:S(2)}, u32[]{:S(2)}) collective-permute-start(bf16[4,128,256]{2,1,0:T(8,128)(2,1)S(1)} %add_convert_fusion), channel_id=1, source_target_pairs={{0,1},{3,2},{1,3},{2,0},{4,5},{7,6},{5,7},{6,4},{8,9},{11,10},{9,1... | collective-permute-start | bytes 786440 | tf_op jit(solution)/shard_map/ppermute | solution.py:125
  71.4 1.6 %correlate.4 = bf16[4,128,256]{2,1,0:T(8,128)(2,1)S(1)} custom-call(s32[3]{0:T(128)S(1)} %get-tuple-element.9.refs_0_, bf16[4,2048]{1,0:T(4,128)(2,1)S(1)} %copy-done, bf16[256,2048]{1,0:T(8,128)(2,1)S(1)} %bitcast.12, bf16[256,2048]{1,0:T(8,128)(2,1)S(1)} %collective-permute-done.refs_3_), custom_call_target="tpu_custom_call" | custom-call | flops 536870912 | bytes 4194304 | tf_op jit(solution)/shard_map/correlate/pallas_call | solution.py:83
  73.0 0.1 collective-permute-done.1
  73.1 0.0 collective-permute-done.4
  73.1 8.3 %collective-permute-done.3 = bf16[4,128,256]{2,1,0:T(8,128)(2,1)S(1)} collective-permute-done((bf16[4,128,256]{2,1,0:T(8,128)(2,1)S(1)}, bf16[4,128,256]{2,1,0:T(8,128)(2,1)S(1)}, u32[]{:S(2)}, u32[]{:S(2)}) %collective-permute-start.3) | collective-permute-done | bytes 262176 | tf_op jit(solution)/shard_map/ppermute | solution.py:125
  81.4 0.2 fusion
  81.6 0.9 %copy.4 = bf16[128,4,256]{2,1,0:T(4,128)(2,1)} copy(bf16[128,4,256]{2,0,1:T(8,128)(2,1)S(1)} %fusion) | data formatting | bytes 524288 | tf_op jit(solution)/shard_map/transpose | solution.py:128
Async XLA Ops:
  47.5 7.4 %collective-permute-start = (bf16[256,2048]{1,0:T(8,128)(2,1)S(1)}, bf16[256,2048]{1,0:T(8,128)(2,1)S(1)}, u32[]{:S(2)}, u32[]{:S(2)}) collective-permute-start(bf16[256,2048]{1,0:T(8,128)(2,1)S(1)} %bitcast.8), channel_id=1, source_target_pairs={{0,4},{4,0},{1,5},{5,1},{2,6},{6,2},{3,7},{7,3},{8,12},{12,8},{9,1... | collective-permute-start | bytes 3145736 | tf_op jit(solution)/shard_map/ppermute | solution.py:108
  52.7 2.2 %copy-start = (bf16[4,2048]{1,0:T(4,128)(2,1)S(1)}, bf16[4,2048]{1,0:T(4,128)(2,1)}, u32[]{:S(2)}) copy-start(bf16[4,2048]{1,0:T(4,128)(2,1)} %get-tuple-element.7.refs_1_) | copy-start | bytes 49156
  56.6 12.8 %collective-permute-start.2 = (bf16[4,128,256]{2,1,0:T(8,128)(2,1)S(1)}, bf16[4,128,256]{2,1,0:T(8,128)(2,1)S(1)}, u32[]{:S(2)}, u32[]{:S(2)}) collective-permute-start(bf16[4,128,256]{2,1,0:T(8,128)(2,1)S(1)} %correlate.7), channel_id=1, source_target_pairs={{0,1},{3,2},{4,5},{7,6},{8,9},{11,10},{12,13},{15,14},{16,17},{19,... | collective-permute-start | bytes 786440 | tf_op jit(solution)/shard_map/ppermute | solution.py:121
  61.7 11.4 %collective-permute-start.4 = (bf16[4,128,256]{2,1,0:T(8,128)(2,1)S(1)}, bf16[4,128,256]{2,1,0:T(8,128)(2,1)S(1)}, u32[]{:S(2)}, u32[]{:S(2)}) collective-permute-start(bf16[4,128,256]{2,1,0:T(8,128)(2,1)S(1)} %correlate.7), channel_id=1, source_target_pairs={{1,2},{2,1},{5,6},{6,5},{9,10},{10,9},{13,14},{14,13},{17,18},{18,... | collective-permute-start | bytes 786440 | tf_op jit(solution)/shard_map/ppermute | solution.py:123
  64.0 9.1 %collective-permute-start.1 = (bf16[4,128,256]{2,1,0:T(8,128)(2,1)S(1)}, bf16[4,128,256]{2,1,0:T(8,128)(2,1)S(1)}, u32[]{:S(2)}, u32[]{:S(2)}) collective-permute-start(bf16[4,128,256]{2,1,0:T(8,128)(2,1)S(1)} %correlate.5), channel_id=1, source_target_pairs={{0,2},{3,1},{1,0},{2,3},{4,6},{7,5},{5,4},{6,7},{8,10},{11,9},{9,8... | collective-permute-start | bytes 786440 | tf_op jit(solution)/shard_map/ppermute | solution.py:120
  69.5 12.0 %collective-permute-start.3 = (bf16[4,128,256]{2,1,0:T(8,128)(2,1)S(1)}, bf16[4,128,256]{2,1,0:T(8,128)(2,1)S(1)}, u32[]{:S(2)}, u32[]{:S(2)}) collective-permute-start(bf16[4,128,256]{2,1,0:T(8,128)(2,1)S(1)} %add_convert_fusion), channel_id=1, source_target_pairs={{0,1},{3,2},{1,3},{2,0},{4,5},{7,6},{5,7},{6,4},{8,9},{11,10},{9,1... | collective-permute-start | bytes 786440 | tf_op jit(solution)/shard_map/ppermute | solution.py:125

commit v9 on v8

--- a/solution.py
+++ b/solution.py
@@ -90,7 +90,7 @@
             pltpu.VMEM((rows * chunk, samples), jnp.bfloat16),
             pltpu.VMEM((cols, samples), jnp.bfloat16),
         ],
-        compiler_params=pltpu.CompilerParams(vmem_limit_bytes=40 * MiB),
+        compiler_params=pltpu.CompilerParams(vmem_limit_bytes=16 * MiB),
         cost_estimate=pl.CostEstimate(
             flops=2 * rows * chunk * samples * cols, bytes_accessed=4 * MiB, transcendentals=0
         ),

time: 83 us -> 83 us (level)
  no operation moved by 1% of the time
where the time goes in v9:
time: 83 us; the launch traced here: 82.5 us
  blocking collectives  45.7 us (55%)
  starting transfers between devices  16.6 us (20%)
  waiting for transfers between devices  9.81 us (12%)
  Pallas kernels  8.16 us (10%)
  local copies, waits for them, and re-layouts  1.09 us (1%)
    all_to_all x1, blocking collectives, local(): lax.all_to_all(sent, ('z', 'yh'), 0, 0, tiled=True)  29.1 us
    all_to_all x1, blocking collectives, local(): lax.all_to_all(sent, 'x', 0, 0, tiled=True).reshape(-1, slab.shape[1])  16.6 us
    ppermute x1, waiting for transfers between devices, local(): last = lax.ppermute(later, 'tm', [(0, 1), (3, 2), (1, 3), (2, 0)])  8.31 us
    pallas_call x4, Pallas kernels, correlate(): pl.pallas_call(lambda *refs: correlate_kernel(rows, *refs), out_shape=jax...  6.54 us
    ppermute x1, starting transfers between devices, local(): other = lax.ppermute(share, 'core', [(0, 1), (1, 0)])  5.17 us
    ppermute x1, starting transfers between devices, local(): passed = lax.ppermute(near, 'tm', [(0, 1), (3, 2)])  5.11 us
    ppermute x1, starting transfers between devices, local(): turned = lax.ppermute(turned, 'tm', [(0, 2), (3, 1), (1, 0), (2, 3)])  3.69 us
    ppermute x1, starting transfers between devices, local(): last = lax.ppermute(later, 'tm', [(0, 1), (3, 2), (1, 3), (2, 0)])  1.92 us
  transfers between devices with their start and end apart: 5, of which 3 were waited for; matrix products, arithmetic and copies ran while one was open for 0% of the time, Pallas kernels for 6%

profile of v9, /device:TPU:1, one launch (start us, length us, event | category | flops | bytes accessed | tf_op | source)
XLA Modules:
  0.0 82.5 jit_solution(14818955802550200567)
XLA Ops:
  0.0 1.6 %normalize.1 = (bf16[4,2048]{1,0:T(4,128)(2,1)}, bf16[16,4,2048]{2,1,0:T(4,128)(2,1)}) custom-call(bf16[1,4,2048]{2,1,0:T(4,128)(2,1)} %records_ref.1, s32[4]{0:T(128)} %alive_ref.1), custom_call_target="tpu_custom_call" | custom-call | tf_op jit(solution)/shard_map/normalize/pallas_call | solution.py:33
  1.6 29.1 %all_to_all.10 = bf16[16,4,2048]{2,1,0:T(4,128)(2,1)S(1)} all-to-all(bf16[16,4,2048]{2,1,0:T(4,128)(2,1)} %get-tuple-element.8), channel_id=1, replica_groups=mesh['x'=4,'z'=8,'yh'=2,'core'=2,'tm'=4] {'z','yh'}, dimensions={0} | all-to-all | bytes 524288 | tf_op jit(solution)/shard_map/all_to_all | solution.py:105
  30.7 0.1 broadcast_in_dim.12
  30.8 0.1 broadcast_in_dim.13
  30.9 16.6 %all_to_all.11 = bf16[4,64,2048]{2,1,0:T(8,128)(2,1)S(1)} all-to-all(bf16[4,64,2048]{2,1,0:T(8,128)(2,1)S(1)} %broadcast_in_dim.13), channel_id=1, replica_groups=mesh['x'=4,'z'=8,'yh'=2,'core'=2,'tm'=4] {'x'}, dimensions={0} | all-to-all | bytes 2097152 | tf_op jit(solution)/shard_map/all_to_all | solution.py:107
  47.5 5.2 %collective-permute-start = (bf16[256,2048]{1,0:T(8,128)(2,1)S(1)}, bf16[256,2048]{1,0:T(8,128)(2,1)S(1)}, u32[]{:S(2)}, u32[]{:S(2)}) collective-permute-start(bf16[256,2048]{1,0:T(8,128)(2,1)S(1)} %bitcast.8), channel_id=1, source_target_pairs={{0,4},{4,0},{1,5},{5,1},{2,6},{6,2},{3,7},{7,3},{8,12},{12,8},{9,1... | collective-permute-start | bytes 3145736 | tf_op jit(solution)/shard_map/ppermute | solution.py:108
  52.7 0.0 copy-start
  53.4 0.1 pad_add_fusion
  53.5 0.1 pad_add_fusion.2
  53.5 1.4 %collective-permute-done.refs_3_ = bf16[256,2048]{1,0:T(8,128)(2,1)S(1)} collective-permute-done((bf16[256,2048]{1,0:T(8,128)(2,1)S(1)}, bf16[256,2048]{1,0:T(8,128)(2,1)S(1)}, u32[]{:S(2)}, u32[]{:S(2)}) %collective-permute-start) | collective-permute-done | bytes 1048608 | tf_op jit(solution)/shard_map/ppermute | solution.py:108
  54.9 0.0 copy-done
  54.9 1.6 %correlate.7 = bf16[4,128,256]{2,1,0:T(8,128)(2,1)S(1)} custom-call(s32[3]{0:T(128)S(1)} %get-tuple-element.13.refs_0_, bf16[4,2048]{1,0:T(4,128)(2,1)S(1)} %copy-done, bf16[256,2048]{1,0:T(8,128)(2,1)S(1)} %bitcast.9, bf16[256,2048]{1,0:T(8,128)(2,1)S(1)} %collective-permute-done.refs_3_), custom_call_target="tpu_custom_call" | custom-call | flops 536870912 | bytes 4194304 | tf_op jit(solution)/shard_map/correlate/pallas_call | solution.py:83
  56.6 5.1 %collective-permute-start.2 = (bf16[4,128,256]{2,1,0:T(8,128)(2,1)S(1)}, bf16[4,128,256]{2,1,0:T(8,128)(2,1)S(1)}, u32[]{:S(2)}, u32[]{:S(2)}) collective-permute-start(bf16[4,128,256]{2,1,0:T(8,128)(2,1)S(1)} %correlate.7), channel_id=1, source_target_pairs={{0,1},{3,2},{4,5},{7,6},{8,9},{11,10},{12,13},{15,14},{16,17},{19,... | collective-permute-start | bytes 786440 | tf_op jit(solution)/shard_map/ppermute | solution.py:121
  61.7 0.7 collective-permute-start.4
  62.4 1.6 %correlate.5 = bf16[4,128,256]{2,1,0:T(8,128)(2,1)S(1)} custom-call(s32[3]{0:T(128)S(1)} %get-tuple-element.11.refs_0_, bf16[4,2048]{1,0:T(4,128)(2,1)S(1)} %copy-done, bf16[256,2048]{1,0:T(8,128)(2,1)S(1)} %bitcast.10, bf16[256,2048]{1,0:T(8,128)(2,1)S(1)} %collective-permute-done.refs_3_), custom_call_target="tpu_custom_call" | custom-call | flops 536870912 | bytes 4194304 | tf_op jit(solution)/shard_map/correlate/pallas_call | solution.py:83
  64.0 3.7 %collective-permute-start.1 = (bf16[4,128,256]{2,1,0:T(8,128)(2,1)S(1)}, bf16[4,128,256]{2,1,0:T(8,128)(2,1)S(1)}, u32[]{:S(2)}, u32[]{:S(2)}) collective-permute-start(bf16[4,128,256]{2,1,0:T(8,128)(2,1)S(1)} %correlate.5), channel_id=1, source_target_pairs={{0,2},{3,1},{1,0},{2,3},{4,6},{7,5},{5,4},{6,7},{8,10},{11,9},{9,8... | collective-permute-start | bytes 786440 | tf_op jit(solution)/shard_map/ppermute | solution.py:120
  67.7 1.6 %correlate.6 = bf16[4,128,256]{2,1,0:T(8,128)(2,1)S(1)} custom-call(s32[3]{0:T(128)S(1)} %get-tuple-element.12.refs_0_, bf16[4,2048]{1,0:T(4,128)(2,1)S(1)} %copy-done, bf16[256,2048]{1,0:T(8,128)(2,1)S(1)} %bitcast.11, bf16[256,2048]{1,0:T(8,128)(2,1)S(1)} %collective-permute-done.refs_3_), custom_call_target="tpu_custom_call" | custom-call | flops 536870912 | bytes 4194304 | tf_op jit(solution)/shard_map/correlate/pallas_call | solution.py:83
  69.4 0.0 collective-permute-done.2
  69.4 0.1 add_convert_fusion
  69.5 1.9 %collective-permute-start.3 = (bf16[4,128,256]{2,1,0:T(8,128)(2,1)S(1)}, bf16[4,128,256]{2,1,0:T(8,128)(2,1)S(1)}, u32[]{:S(2)}, u32[]{:S(2)}) collective-permute-start(bf16[4,128,256]{2,1,0:T(8,128)(2,1)S(1)} %add_convert_fusion), channel_id=1, source_target_pairs={{0,1},{3,2},{1,3},{2,0},{4,5},{7,6},{5,7},{6,4},{8,9},{11,10},{9,1... | collective-permute-start | bytes 786440 | tf_op jit(solution)/shard_map/ppermute | solution.py:125
  71.4 1.6 %correlate.4 = bf16[4,128,256]{2,1,0:T(8,128)(2,1)S(1)} custom-call(s32[3]{0:T(128)S(1)} %get-tuple-element.9.refs_0_, bf16[4,2048]{1,0:T(4,128)(2,1)S(1)} %copy-done, bf16[256,2048]{1,0:T(8,128)(2,1)S(1)} %bitcast.12, bf16[256,2048]{1,0:T(8,128)(2,1)S(1)} %collective-permute-done.refs_3_), custom_call_target="tpu_custom_call" | custom-call | flops 536870912 | bytes 4194304 | tf_op jit(solution)/shard_map/correlate/pallas_call | solution.py:83
  73.0 0.1 collective-permute-done.1
  73.1 0.0 collective-permute-done.4
  73.1 8.3 %collective-permute-done.3 = bf16[4,128,256]{2,1,0:T(8,128)(2,1)S(1)} collective-permute-done((bf16[4,128,256]{2,1,0:T(8,128)(2,1)S(1)}, bf16[4,128,256]{2,1,0:T(8,128)(2,1)S(1)}, u32[]{:S(2)}, u32[]{:S(2)}) %collective-permute-start.3) | collective-permute-done | bytes 262176 | tf_op jit(solution)/shard_map/ppermute | solution.py:125
  81.4 0.2 fusion
  81.6 0.9 %copy.4 = bf16[128,4,256]{2,1,0:T(4,128)(2,1)} copy(bf16[128,4,256]{2,0,1:T(8,128)(2,1)S(1)} %fusion) | data formatting | bytes 524288 | tf_op jit(solution)/shard_map/transpose | solution.py:128
Async XLA Ops:
  47.5 7.4 %collective-permute-start = (bf16[256,2048]{1,0:T(8,128)(2,1)S(1)}, bf16[256,2048]{1,0:T(8,128)(2,1)S(1)}, u32[]{:S(2)}, u32[]{:S(2)}) collective-permute-start(bf16[256,2048]{1,0:T(8,128)(2,1)S(1)} %bitcast.8), channel_id=1, source_target_pairs={{0,4},{4,0},{1,5},{5,1},{2,6},{6,2},{3,7},{7,3},{8,12},{12,8},{9,1... | collective-permute-start | bytes 3145736 | tf_op jit(solution)/shard_map/ppermute | solution.py:108
  52.7 2.2 %copy-start = (bf16[4,2048]{1,0:T(4,128)(2,1)S(1)}, bf16[4,2048]{1,0:T(4,128)(2,1)}, u32[]{:S(2)}) copy-start(bf16[4,2048]{1,0:T(4,128)(2,1)} %get-tuple-element.7.refs_1_) | copy-start | bytes 49156
  56.6 12.8 %collective-permute-start.2 = (bf16[4,128,256]{2,1,0:T(8,128)(2,1)S(1)}, bf16[4,128,256]{2,1,0:T(8,128)(2,1)S(1)}, u32[]{:S(2)}, u32[]{:S(2)}) collective-permute-start(bf16[4,128,256]{2,1,0:T(8,128)(2,1)S(1)} %correlate.7), channel_id=1, source_target_pairs={{0,1},{3,2},{4,5},{7,6},{8,9},{11,10},{12,13},{15,14},{16,17},{19,... | collective-permute-start | bytes 786440 | tf_op jit(solution)/shard_map/ppermute | solution.py:121
  61.7 11.4 %collective-permute-start.4 = (bf16[4,128,256]{2,1,0:T(8,128)(2,1)S(1)}, bf16[4,128,256]{2,1,0:T(8,128)(2,1)S(1)}, u32[]{:S(2)}, u32[]{:S(2)}) collective-permute-start(bf16[4,128,256]{2,1,0:T(8,128)(2,1)S(1)} %correlate.7), channel_id=1, source_target_pairs={{1,2},{2,1},{5,6},{6,5},{9,10},{10,9},{13,14},{14,13},{17,18},{18,... | collective-permute-start | bytes 786440 | tf_op jit(solution)/shard_map/ppermute | solution.py:123
  64.0 9.1 %collective-permute-start.1 = (bf16[4,128,256]{2,1,0:T(8,128)(2,1)S(1)}, bf16[4,128,256]{2,1,0:T(8,128)(2,1)S(1)}, u32[]{:S(2)}, u32[]{:S(2)}) collective-permute-start(bf16[4,128,256]{2,1,0:T(8,128)(2,1)S(1)} %correlate.5), channel_id=1, source_target_pairs={{0,2},{3,1},{1,0},{2,3},{4,6},{7,5},{5,4},{6,7},{8,10},{11,9},{9,8... | collective-permute-start | bytes 786440 | tf_op jit(solution)/shard_map/ppermute | solution.py:120
  69.5 12.0 %collective-permute-start.3 = (bf16[4,128,256]{2,1,0:T(8,128)(2,1)S(1)}, bf16[4,128,256]{2,1,0:T(8,128)(2,1)S(1)}, u32[]{:S(2)}, u32[]{:S(2)}) collective-permute-start(bf16[4,128,256]{2,1,0:T(8,128)(2,1)S(1)} %add_convert_fusion), channel_id=1, source_target_pairs={{0,1},{3,2},{1,3},{2,0},{4,5},{7,6},{5,7},{6,4},{8,9},{11,10},{9,1... | collective-permute-start | bytes 786440 | tf_op jit(solution)/shard_map/ppermute | solution.py:125

commit v10 on v9

--- a/solution.py
+++ b/solution.py
@@ -51,7 +51,8 @@
     last = LAGS // chunk - 1
     block, core = where_ref[0], where_ref[1]
     start = pl.multiple_of(chunk * (last - where_ref[2]), chunk)
-    line_ref[...] = jnp.zeros(line_ref.shape, jnp.float32)
+    for edge in (0, 2 * chunk + samples):
+        line_ref[:, pl.ds(edge, 2 * chunk)] = jnp.zeros((rows, 2 * chunk), jnp.float32)
     line_ref[:, pl.ds(2 * chunk, samples)] = own_ref[...].astype(jnp.float32)
     for c in range(rows):
         line = line_ref[pl.ds(c, 1), pl.ds(start, samples + chunk)]

time: 83 us -> 83 us (level)
  no operation moved by 1% of the time
where the time goes in v10:
time: 83 us; the launch traced here: 82.5 us
  blocking collectives  45.7 us (55%)
  starting transfers between devices  16.6 us (20%)
  waiting for transfers between devices  9.81 us (12%)
  Pallas kernels  8.16 us (10%)
  local copies, waits for them, and re-layouts  1.09 us (1%)
    all_to_all x1, blocking collectives, local(): lax.all_to_all(sent, ('z', 'yh'), 0, 0, tiled=True)  29.1 us
    all_to_all x1, blocking collectives, local(): lax.all_to_all(sent, 'x', 0, 0, tiled=True).reshape(-1, slab.shape[1])  16.6 us
    ppermute x1, waiting for transfers between devices, local(): last = lax.ppermute(later, 'tm', [(0, 1), (3, 2), (1, 3), (2, 0)])  8.31 us
    pallas_call x4, Pallas kernels, correlate(): pl.pallas_call(lambda *refs: correlate_kernel(rows, *refs), out_shape=jax...  6.54 us
    ppermute x1, starting transfers between devices, local(): other = lax.ppermute(share, 'core', [(0, 1), (1, 0)])  5.17 us
    ppermute x1, starting transfers between devices, local(): passed = lax.ppermute(near, 'tm', [(0, 1), (3, 2)])  5.11 us
    ppermute x1, starting transfers between devices, local(): turned = lax.ppermute(turned, 'tm', [(0, 2), (3, 1), (1, 0), (2, 3)])  3.69 us
    ppermute x1, starting transfers between devices, local(): last = lax.ppermute(later, 'tm', [(0, 1), (3, 2), (1, 3), (2, 0)])  1.92 us
  transfers between devices with their start and end apart: 5, of which 3 were waited for; matrix products, arithmetic and copies ran while one was open for 0% of the time, Pallas kernels for 6%

profile of v10, /device:TPU:1, one launch (start us, length us, event | category | flops | bytes accessed | tf_op | source)
XLA Modules:
  0.0 82.5 jit_solution(14818955802550200567)
XLA Ops:
  0.0 1.6 %normalize.1 = (bf16[4,2048]{1,0:T(4,128)(2,1)}, bf16[16,4,2048]{2,1,0:T(4,128)(2,1)}) custom-call(bf16[1,4,2048]{2,1,0:T(4,128)(2,1)} %records_ref.1, s32[4]{0:T(128)} %alive_ref.1), custom_call_target="tpu_custom_call" | custom-call | tf_op jit(solution)/shard_map/normalize/pallas_call | solution.py:33
  1.6 29.1 %all_to_all.10 = bf16[16,4,2048]{2,1,0:T(4,128)(2,1)S(1)} all-to-all(bf16[16,4,2048]{2,1,0:T(4,128)(2,1)} %get-tuple-element.8), channel_id=1, replica_groups=mesh['x'=4,'z'=8,'yh'=2,'core'=2,'tm'=4] {'z','yh'}, dimensions={0} | all-to-all | bytes 524288 | tf_op jit(solution)/shard_map/all_to_all | solution.py:106
  30.7 0.1 broadcast_in_dim.12
  30.8 0.1 broadcast_in_dim.13
  30.9 16.6 %all_to_all.11 = bf16[4,64,2048]{2,1,0:T(8,128)(2,1)S(1)} all-to-all(bf16[4,64,2048]{2,1,0:T(8,128)(2,1)S(1)} %broadcast_in_dim.13), channel_id=1, replica_groups=mesh['x'=4,'z'=8,'yh'=2,'core'=2,'tm'=4] {'x'}, dimensions={0} | all-to-all | bytes 2097152 | tf_op jit(solution)/shard_map/all_to_all | solution.py:108
  47.5 5.2 %collective-permute-start = (bf16[256,2048]{1,0:T(8,128)(2,1)S(1)}, bf16[256,2048]{1,0:T(8,128)(2,1)S(1)}, u32[]{:S(2)}, u32[]{:S(2)}) collective-permute-start(bf16[256,2048]{1,0:T(8,128)(2,1)S(1)} %bitcast.8), channel_id=1, source_target_pairs={{0,4},{4,0},{1,5},{5,1},{2,6},{6,2},{3,7},{7,3},{8,12},{12,8},{9,1... | collective-permute-start | bytes 3145736 | tf_op jit(solution)/shard_map/ppermute | solution.py:109
  52.7 0.0 copy-start
  53.4 0.1 pad_add_fusion
  53.5 0.1 pad_add_fusion.2
  53.5 1.4 %collective-permute-done.refs_3_ = bf16[256,2048]{1,0:T(8,128)(2,1)S(1)} collective-permute-done((bf16[256,2048]{1,0:T(8,128)(2,1)S(1)}, bf16[256,2048]{1,0:T(8,128)(2,1)S(1)}, u32[]{:S(2)}, u32[]{:S(2)}) %collective-permute-start) | collective-permute-done | bytes 1048608 | tf_op jit(solution)/shard_map/ppermute | solution.py:109
  54.9 0.0 copy-done
  54.9 1.6 %correlate.7 = bf16[4,128,256]{2,1,0:T(8,128)(2,1)S(1)} custom-call(s32[3]{0:T(128)S(1)} %get-tuple-element.13.refs_0_, bf16[4,2048]{1,0:T(4,128)(2,1)S(1)} %copy-done, bf16[256,2048]{1,0:T(8,128)(2,1)S(1)} %bitcast.9, bf16[256,2048]{1,0:T(8,128)(2,1)S(1)} %collective-permute-done.refs_3_), custom_call_target="tpu_custom_call" | custom-call | flops 536870912 | bytes 4194304 | tf_op jit(solution)/shard_map/correlate/pallas_call | solution.py:84
  56.6 5.1 %collective-permute-start.2 = (bf16[4,128,256]{2,1,0:T(8,128)(2,1)S(1)}, bf16[4,128,256]{2,1,0:T(8,128)(2,1)S(1)}, u32[]{:S(2)}, u32[]{:S(2)}) collective-permute-start(bf16[4,128,256]{2,1,0:T(8,128)(2,1)S(1)} %correlate.7), channel_id=1, source_target_pairs={{0,1},{3,2},{4,5},{7,6},{8,9},{11,10},{12,13},{15,14},{16,17},{19,... | collective-permute-start | bytes 786440 | tf_op jit(solution)/shard_map/ppermute | solution.py:122
  61.7 0.7 collective-permute-start.4
  62.4 1.6 %correlate.5 = bf16[4,128,256]{2,1,0:T(8,128)(2,1)S(1)} custom-call(s32[3]{0:T(128)S(1)} %get-tuple-element.11.refs_0_, bf16[4,2048]{1,0:T(4,128)(2,1)S(1)} %copy-done, bf16[256,2048]{1,0:T(8,128)(2,1)S(1)} %bitcast.10, bf16[256,2048]{1,0:T(8,128)(2,1)S(1)} %collective-permute-done.refs_3_), custom_call_target="tpu_custom_call" | custom-call | flops 536870912 | bytes 4194304 | tf_op jit(solution)/shard_map/correlate/pallas_call | solution.py:84
  64.0 3.7 %collective-permute-start.1 = (bf16[4,128,256]{2,1,0:T(8,128)(2,1)S(1)}, bf16[4,128,256]{2,1,0:T(8,128)(2,1)S(1)}, u32[]{:S(2)}, u32[]{:S(2)}) collective-permute-start(bf16[4,128,256]{2,1,0:T(8,128)(2,1)S(1)} %correlate.5), channel_id=1, source_target_pairs={{0,2},{3,1},{1,0},{2,3},{4,6},{7,5},{5,4},{6,7},{8,10},{11,9},{9,8... | collective-permute-start | bytes 786440 | tf_op jit(solution)/shard_map/ppermute | solution.py:121
  67.7 1.6 %correlate.6 = bf16[4,128,256]{2,1,0:T(8,128)(2,1)S(1)} custom-call(s32[3]{0:T(128)S(1)} %get-tuple-element.12.refs_0_, bf16[4,2048]{1,0:T(4,128)(2,1)S(1)} %copy-done, bf16[256,2048]{1,0:T(8,128)(2,1)S(1)} %bitcast.11, bf16[256,2048]{1,0:T(8,128)(2,1)S(1)} %collective-permute-done.refs_3_), custom_call_target="tpu_custom_call" | custom-call | flops 536870912 | bytes 4194304 | tf_op jit(solution)/shard_map/correlate/pallas_call | solution.py:84
  69.4 0.0 collective-permute-done.2
  69.4 0.1 add_convert_fusion
  69.5 1.9 %collective-permute-start.3 = (bf16[4,128,256]{2,1,0:T(8,128)(2,1)S(1)}, bf16[4,128,256]{2,1,0:T(8,128)(2,1)S(1)}, u32[]{:S(2)}, u32[]{:S(2)}) collective-permute-start(bf16[4,128,256]{2,1,0:T(8,128)(2,1)S(1)} %add_convert_fusion), channel_id=1, source_target_pairs={{0,1},{3,2},{1,3},{2,0},{4,5},{7,6},{5,7},{6,4},{8,9},{11,10},{9,1... | collective-permute-start | bytes 786440 | tf_op jit(solution)/shard_map/ppermute | solution.py:126
  71.4 1.6 %correlate.4 = bf16[4,128,256]{2,1,0:T(8,128)(2,1)S(1)} custom-call(s32[3]{0:T(128)S(1)} %get-tuple-element.9.refs_0_, bf16[4,2048]{1,0:T(4,128)(2,1)S(1)} %copy-done, bf16[256,2048]{1,0:T(8,128)(2,1)S(1)} %bitcast.12, bf16[256,2048]{1,0:T(8,128)(2,1)S(1)} %collective-permute-done.refs_3_), custom_call_target="tpu_custom_call" | custom-call | flops 536870912 | bytes 4194304 | tf_op jit(solution)/shard_map/correlate/pallas_call | solution.py:84
  73.0 0.1 collective-permute-done.1
  73.1 0.0 collective-permute-done.4
  73.1 8.3 %collective-permute-done.3 = bf16[4,128,256]{2,1,0:T(8,128)(2,1)S(1)} collective-permute-done((bf16[4,128,256]{2,1,0:T(8,128)(2,1)S(1)}, bf16[4,128,256]{2,1,0:T(8,128)(2,1)S(1)}, u32[]{:S(2)}, u32[]{:S(2)}) %collective-permute-start.3) | collective-permute-done | bytes 262176 | tf_op jit(solution)/shard_map/ppermute | solution.py:126
  81.4 0.2 fusion
  81.6 0.9 %copy.4 = bf16[128,4,256]{2,1,0:T(4,128)(2,1)} copy(bf16[128,4,256]{2,0,1:T(8,128)(2,1)S(1)} %fusion) | data formatting | bytes 524288 | tf_op jit(solution)/shard_map/transpose | solution.py:129
Async XLA Ops:
  47.5 7.4 %collective-permute-start = (bf16[256,2048]{1,0:T(8,128)(2,1)S(1)}, bf16[256,2048]{1,0:T(8,128)(2,1)S(1)}, u32[]{:S(2)}, u32[]{:S(2)}) collective-permute-start(bf16[256,2048]{1,0:T(8,128)(2,1)S(1)} %bitcast.8), channel_id=1, source_target_pairs={{0,4},{4,0},{1,5},{5,1},{2,6},{6,2},{3,7},{7,3},{8,12},{12,8},{9,1... | collective-permute-start | bytes 3145736 | tf_op jit(solution)/shard_map/ppermute | solution.py:109
  52.7 2.2 %copy-start = (bf16[4,2048]{1,0:T(4,128)(2,1)S(1)}, bf16[4,2048]{1,0:T(4,128)(2,1)}, u32[]{:S(2)}) copy-start(bf16[4,2048]{1,0:T(4,128)(2,1)} %get-tuple-element.7.refs_1_) | copy-start | bytes 49156
  56.6 12.8 %collective-permute-start.2 = (bf16[4,128,256]{2,1,0:T(8,128)(2,1)S(1)}, bf16[4,128,256]{2,1,0:T(8,128)(2,1)S(1)}, u32[]{:S(2)}, u32[]{:S(2)}) collective-permute-start(bf16[4,128,256]{2,1,0:T(8,128)(2,1)S(1)} %correlate.7), channel_id=1, source_target_pairs={{0,1},{3,2},{4,5},{7,6},{8,9},{11,10},{12,13},{15,14},{16,17},{19,... | collective-permute-start | bytes 786440 | tf_op jit(solution)/shard_map/ppermute | solution.py:122
  61.7 11.4 %collective-permute-start.4 = (bf16[4,128,256]{2,1,0:T(8,128)(2,1)S(1)}, bf16[4,128,256]{2,1,0:T(8,128)(2,1)S(1)}, u32[]{:S(2)}, u32[]{:S(2)}) collective-permute-start(bf16[4,128,256]{2,1,0:T(8,128)(2,1)S(1)} %correlate.7), channel_id=1, source_target_pairs={{1,2},{2,1},{5,6},{6,5},{9,10},{10,9},{13,14},{14,13},{17,18},{18,... | collective-permute-start | bytes 786440 | tf_op jit(solution)/shard_map/ppermute | solution.py:124
  64.0 9.1 %collective-permute-start.1 = (bf16[4,128,256]{2,1,0:T(8,128)(2,1)S(1)}, bf16[4,128,256]{2,1,0:T(8,128)(2,1)S(1)}, u32[]{:S(2)}, u32[]{:S(2)}) collective-permute-start(bf16[4,128,256]{2,1,0:T(8,128)(2,1)S(1)} %correlate.5), channel_id=1, source_target_pairs={{0,2},{3,1},{1,0},{2,3},{4,6},{7,5},{5,4},{6,7},{8,10},{11,9},{9,8... | collective-permute-start | bytes 786440 | tf_op jit(solution)/shard_map/ppermute | solution.py:121
  69.5 12.0 %collective-permute-start.3 = (bf16[4,128,256]{2,1,0:T(8,128)(2,1)S(1)}, bf16[4,128,256]{2,1,0:T(8,128)(2,1)S(1)}, u32[]{:S(2)}, u32[]{:S(2)}) collective-permute-start(bf16[4,128,256]{2,1,0:T(8,128)(2,1)S(1)} %add_convert_fusion), channel_id=1, source_target_pairs={{0,1},{3,2},{1,3},{2,0},{4,5},{7,6},{5,7},{6,4},{8,9},{11,10},{9,1... | collective-permute-start | bytes 786440 | tf_op jit(solution)/shard_map/ppermute | solution.py:126
